TPU v7x, 128 devices: a whole 4x4x4 slice. The times are simulated.
128 devices in a mesh: ia: 16 (over z, x_hi, core), ja: 8 (over y, x_lo).
Axes of the slice: x: 4 (x_hi: 2, x_lo: 2; x = x_hi * 2 + x_lo), y: 4, z: 4, core: 2. Of those that a mesh axis runs over, the one named last changes fastest.
Arguments:
- heat_centre_value: float32 [16, 1024, 2048], P(None, 'ja', 'ia'), may hold values from -6 to 6
- saltiness_centre: float32 [16, 1024, 2048], P(None, 'ja', 'ia'), may hold values from -6 to 6
- easting_transport_ratio: float32 [16, 1024, 2048], P(None, 'ja', 'ia'), may hold values from -0.25 to 0.25
- northing_transport_ratio: float32 [16, 1024, 2048], P(None, 'ja', 'ia'), may hold values from -0.25 to 0.25
- sinking_transport_ratio: float32 [16, 1024, 2048], P(None, 'ja', 'ia'), may hold values from -0.15 to 0.15
- spreading_number: float32 [16, 1024, 2048], P(None, 'ja', 'ia'), may hold values from 0.01 to 0.08
- seawater_indicator: int32 [1024, 2048], P('ja', 'ia'), may hold values 0 or 1
- bottom_water_layer: int32 [1024, 2048], P('ja', 'ia'), may hold values from 1 to 16
Outputs:
- temperature_new: float32 [16, 1024, 2048], P(None, 'ja', 'ia')
- salinity_new: float32 [16, 1024, 2048], P(None, 'ja', 'ia')
All inputs are finite; a program needn't handle non-finite values. No bound on the sum of `seawater_indicator` on one device may be relied on, other than what follows from the above.
Results may differ from a plain program's by a relative error of at most 0.0003.
Values sent between devices are 32-bit elements; how exact they have to be, the bound alone decides.
A program may use at most 256 MiB of HBM per device.

v0:
```python
import jax
import jax.numpy as jnp
from jax import lax
from jax.experimental import pallas as pl
from jax.experimental.pallas import tpu as pltpu
from jax.sharding import PartitionSpec as P

NK = 16
NJ = 16
NS = 8
NL = 128
F32 = jnp.float32
EAST, WEST = 0, 1
SOUTH, NORTH = 0, 1


def limiter(centred, a, b):
    upper = jnp.maximum(jnp.minimum(a, b), 0.0)
    lower = jnp.minimum(jnp.maximum(a, b), 0.0)
    return jnp.maximum(jnp.minimum(centred, upper), lower)


def quarter_edge(s):
    a = jnp.abs(s)
    return a * (0.25 - 0.25 * a)


def kernel(
    t_hbm, s_hbm, u_hbm, v_hbm, w_hbm, k_hbm, sea_hbm, bot_hbm,
    tout_hbm, sout_hbm,
    q0, q1, ob, ub, wb, vb, kb, seab, botb, flb,
    ox, sx, bx, ex, oy, sy, by, ey, oz, sz, ez,
    ax, dy, hy, fy,
    hq, hk, hv, hs, hb,
    pq, pr, uko, ukr, flo, flr, cc,
    eo, es, eb, ec, ed,
    in_sem, out_sem, row_send, row_recv, row2_send, row2_recv,
    col_send, col_recv, col2_send, col2_recv,
):
    ia = lax.axis_index("ia")
    ja = lax.axis_index("ja")
    n_ia = lax.axis_size("ia")
    n_ja = lax.axis_size("ja")
    top = ja == n_ja - 1
    low = ja > 0
    east = {"ia": lax.rem(ia + 1, n_ia), "ja": ja}
    west = {"ia": lax.rem(ia + n_ia - 1, n_ia), "ja": ja}
    north = {"ia": jnp.where(top, n_ia - 1 - ia, ia), "ja": jnp.where(top, ja, ja + 1)}
    south = {"ia": ia, "ja": jnp.maximum(ja - 1, 0)}
    nslot = jnp.where(top, NORTH, SOUTH)
    mesh_ids = pl.DeviceIdType.MESH

    lane = lax.broadcasted_iota(jnp.int32, (NS, NL), 1)
    sub = lax.broadcasted_iota(jnp.int32, (NS, NL), 0)
    l4 = lane & 3
    group = lane >> 2
    edge_lanes = ((lane + 2) & (NL - 1)) < 4

    barrier = pltpu.get_barrier_semaphore()
    for device in (east, west, north):
        pl.semaphore_signal(barrier, inc=1, device_id=device, device_id_type=mesh_ids)

    @pl.when(low)
    def _():
        pl.semaphore_signal(barrier, inc=1, device_id=south, device_id_type=mesh_ids)

    def load(index, src, dst3, lead):
        for s in range(NS):
            rows = pl.ds(NJ * s, NJ)
            if lead:
                pltpu.make_async_copy(src.at[:, rows, :], dst3(s), in_sem.at[index]).start()
            else:
                pltpu.make_async_copy(src.at[rows, :], dst3(s), in_sem.at[index]).start()

    load(0, t_hbm, lambda s: q0.at[0, :, pl.ds(2, NJ), s, :], True)
    load(1, s_hbm, lambda s: q0.at[1, :, pl.ds(2, NJ), s, :], True)
    load(2, sea_hbm, lambda s: seab.at[pl.ds(2, NJ), s, :], False)
    load(3, bot_hbm, lambda s: botb.at[pl.ds(2, NJ), s, :], False)
    load(4, u_hbm, lambda s: ub.at[:, :, s, :], True)
    load(5, k_hbm, lambda s: kb.at[:, pl.ds(1, NJ), s, :], True)
    load(6, v_hbm, lambda s: vb.at[:, pl.ds(1, NJ), s, :], True)
    load(7, w_hbm, lambda s: wb.at[:, :, s, :], True)

    def loaded(index, whole):
        pltpu.make_async_copy(whole, whole, in_sem.at[index]).wait()

    pl.semaphore_wait(barrier, jnp.where(low, 4, 3))

    def remote(src, dst, ssem, rsem, device):
        return pltpu.make_async_remote_copy(
            src_ref=src, dst_ref=dst, send_sem=ssem, recv_sem=rsem,
            device_id=device, device_id_type=mesh_ids,
        )

    def row_copies(first, last, slot, direction, device):
        pair = pl.ds(first, 2)
        line = pl.ds(last, 1)
        parts = [
            (t_hbm.at[:, pair, :], hq.at[0, slot, 0, :, :, 0, :]),
            (s_hbm.at[:, pair, :], hq.at[0, slot, 1, :, :, 0, :]),
            (k_hbm.at[:, line, :], hk.at[slot, :, :, 0, :]),
            (v_hbm.at[:, line, :], hv.at[slot, :, :, 0, :]),
            (sea_hbm.at[pair, :], hs.at[slot, :, 0, :]),
            (bot_hbm.at[pair, :], hb.at[slot, :, 0, :]),
        ]
        return [
            remote(src, dst, row_send.at[direction, n], row_recv.at[slot, n], device)
            for n, (src, dst) in enumerate(parts)
        ]

    rows_total = NJ * NS

    def north_rows(slot):
        return row_copies(rows_total - 2, rows_total - 1, slot, 0, north)

    def south_rows():
        return row_copies(0, 0, NORTH, 1, south)

    for copy in north_rows(nslot):
        copy.start()

    @pl.when(low)
    def _():
        for copy in south_rows():
            copy.start()

    def pack(load_vreg, count):
        acc = jnp.zeros((NS, NL), F32)
        for n in range(count):
            moved = pltpu.roll(load_vreg(n), (4 * n + 2) % NL, 1)
            acc = jnp.where(group == n, moved, acc)
        return acc

    def col_copies(step, part):
        first, size = ((2, 8), (10, 6), (0, 2))[part]
        sl = pl.ds(first, size)
        return [
            remote(pq.at[step, sl], pr.at[step, EAST, sl], col2_send.at[step, 0, part], col2_recv.at[step, EAST, part], west),
            remote(pq.at[step, sl], pr.at[step, WEST, sl], col2_send.at[step, 1, part], col2_recv.at[step, WEST, part], east),
        ]

    def static_col_copies():
        return [
            remote(uko, ukr.at[EAST], col_send.at[0, 0], col_recv.at[EAST, 0], west),
            remote(uko, ukr.at[WEST], col_send.at[1, 0], col_recv.at[WEST, 0], east),
            remote(flo, flr.at[EAST], col_send.at[0, 1], col_recv.at[EAST, 1], west),
            remote(flo, flr.at[WEST], col_send.at[1, 1], col_recv.at[WEST, 1], east),
        ]

    loaded(0, q0.at[0, :, pl.ds(2, NJ)])
    loaded(1, q0.at[1, :, pl.ds(2, NJ)])

    @pl.loop(0, NJ // 2)
    def _(half):
        for h in range(2):
            j = 2 * half + h
            pq[0, j] = pack(lambda n: q0[n // NK, n % NK, j + 2], 2 * NK)

    for part in range(3):
        for copy in col_copies(0, part):
            copy.start()

    loaded(2, seab.at[pl.ds(2, NJ)])
    loaded(3, botb.at[pl.ds(2, NJ)])
    for j in range(2, NJ + 2):
        flb[j] = (seab[j] * botb[j]).astype(F32)
    flo[...] = pack(lambda n: flb[n + 2], NJ)
    loaded(4, ub)
    loaded(5, kb.at[:, pl.ds(1, NJ)])

    @pl.loop(0, NJ // 2)
    def _(half):
        for h in range(2):
            j = 2 * half + h
            uko[j] = pack(lambda n: ub[n, j] if n < NK else kb[n - NK, j + 1], 2 * NK)

    for copy in static_col_copies():
        copy.start()

    loaded(6, vb.at[:, pl.ds(1, NJ)])
    loaded(7, wb)

    def open_y(j):
        face = jnp.minimum(flb[j + 2], flb[j + 3])
        for k in range(NK):
            oy[k, j + 2] = jnp.where(face > k, 4.0, 0.0)

    def coef_y(j):
        face = jnp.minimum(flb[j + 2], flb[j + 3])
        for k in range(NK):
            v = vb[k, j + 1]
            sy[k, j + 1] = jnp.where(face > k, v, 0.0)
            by[k, j + 1] = jnp.minimum(0.25 * v, 0.0) - 0.125 * (kb[k, j + 1] + kb[k, j + 2])
            ey[k, j + 1] = quarter_edge(v)

    @pl.loop(0, NJ)
    def _(j):
        fl = flb[j + 2]
        face = jnp.where(lane == NL - 1, 0.0, jnp.minimum(fl, pltpu.roll(fl, NL - 1, 1)))
        for k in range(NK):
            is_open = face > k
            u = ub[k, j]
            kap = kb[k, j + 1]
            ox[k, j] = jnp.where(is_open, 4.0, 0.0)
            sx[k, j] = jnp.where(is_open, u, 0.0)
            bx[k, j] = jnp.minimum(0.25 * u, 0.0) - 0.125 * (kap + pltpu.roll(kap, NL - 1, 1))
            ex[k, j] = quarter_edge(u)
            if k < NK - 1:
                below = fl > k + 1
                w = wb[k, j]
                oz[k, j] = jnp.where(below, 4.0, 0.0)
                sz[k, j] = jnp.where(below, w, 0.0)
                ez[k, j] = quarter_edge(w)

    @pl.loop(0, NJ - 1)
    def _(j):
        open_y(j)
        coef_y(j)

    south_sub = (sub == 0) & low
    north_sub = sub == 0

    def mirror(x):
        return jnp.take_along_axis(x, NL - 1 - lane, axis=1)

    def from_south(halo, own):
        return jnp.where(south_sub, halo, pltpu.roll(own, 1, 0))

    def from_north(halo, own):
        return pltpu.roll(jnp.where(north_sub, halo, own), NS - 1, 0)

    def fold_q(step):
        @pl.when(top)
        def _():
            for t in range(2):
                @pl.loop(0, NK // 4)
                def _(kk):
                    for k4 in range(4):
                        k = 4 * kk + k4
                        near = mirror(hq[step, NORTH, t, k, 1])
                        far = mirror(hq[step, NORTH, t, k, 0])
                        hq[step, NORTH, t, k, 0] = near
                        hq[step, NORTH, t, k, 1] = far

    def halo_q(step, q):
        fold_q(step)

        @pl.loop(0, NK // 4)
        def _(kk):
            for k4 in range(4):
                k = 4 * kk + k4
                for t in range(2):
                    for r in range(2):
                        q[t, k, r] = from_south(hq[step, SOUTH, t, k, r], q[t, k, NJ + r])
                        q[t, k, NJ + 2 + r] = from_north(hq[step, NORTH, t, k, r], q[t, k, 2 + r])

    def wait_rows(slot):
        for copy in (row_copies(0, 0, slot, 0, north)):
            copy.wait_recv()

    wait_rows(NORTH)

    @pl.when(low)
    def _():
        wait_rows(SOUTH)

    @pl.when(top)
    def _():
        for k in range(NK):
            hk[NORTH, k, 0] = mirror(hk[NORTH, k, 0])
        for h in (hs, hb):
            near = mirror(h[NORTH, 1])
            far = mirror(h[NORTH, 0])
            h[NORTH, 0] = near
            h[NORTH, 1] = far

    for r in range(2):
        south_floor = (hs[SOUTH, r] * hb[SOUTH, r]).astype(F32)
        north_floor = (hs[NORTH, r] * hb[NORTH, r]).astype(F32)
        flb[r] = jnp.where(
            sub == 0, jnp.where(low, south_floor, 0.0), pltpu.roll(flb[NJ + r], 1, 0)
        )
        flb[NJ + 2 + r] = from_north(north_floor, flb[2 + r])
    for k in range(NK):
        kb[k, 0] = from_south(hk[SOUTH, k, 0], kb[k, NJ])
        kb[k, NJ + 1] = from_north(hk[NORTH, k, 0], kb[k, 1])
        vb[k, 0] = from_south(hv[SOUTH, k, 0], vb[k, NJ])
    for j in (-2, -1, NJ - 1, NJ):
        open_y(j)
    for j in (-1, NJ - 1):
        coef_y(j)
    halo_q(0, q0)

    for copy in static_col_copies():
        copy.wait_recv()

    level4 = (group & (NK - 1)).astype(F32)

    @pl.loop(0, NJ // 4)
    def _(quarter):
        for j4 in range(4):
            j = 4 * quarter + j4
            index = 4 * j + l4

            def spread(x):
                return jnp.take_along_axis(x, index, axis=1)

            own_f, east_f, west_f = spread(flo[...]), spread(flr[EAST]), spread(flr[WEST])

            def halves(x):
                other = pltpu.roll(x, NL // 2, 1)
                return jnp.where(lane < NL // 2, x, other), jnp.where(lane < NL // 2, other, x)

            own_u, own_k = halves(uko[j])
            _, east_k = halves(ukr[EAST, j])
            west_u, west_k = halves(ukr[WEST, j])
            first = l4 < 2
            for side in (EAST, WEST):
                if side == EAST:
                    floor, u, kap = jnp.where(first, own_f, east_f), own_u, jnp.where(first, own_k, east_k)
                else:
                    floor, u, kap = (
                        jnp.where(first, west_f, own_f),
                        jnp.where(first, west_u, own_u),
                        jnp.where(first, west_k, own_k),
                    )
                face = jnp.minimum(floor, pltpu.roll(floor, NL - 1, 1))
                is_open = (face > level4) & (l4 < 3)
                b = jnp.minimum(0.25 * u, 0.0) - 0.125 * (kap + pltpu.roll(kap, NL - 1, 1))
                e = quarter_edge(u)
                outer = l4 == 1
                eo[side, j] = jnp.where(is_open, 4.0, 0.0)
                es[side, j] = jnp.where(is_open & outer, u, 0.0)
                eb[side, j] = jnp.where(outer, b, 0.0)
                if side == EAST:
                    c_lanes, d_lanes = outer, first
                else:
                    c_lanes, d_lanes = (l4 == 1) | (l4 == 2), outer
                ec[side, j] = jnp.where((u > 0) & c_lanes, e, 0.0)
                ed[side, j] = jnp.where((u <= 0) & d_lanes, e, 0.0)

    def edge_correction(step, j):
        own = pq[step, j]
        first = l4 < 2
        sums = []
        for side in (EAST, WEST):
            if side == EAST:
                win = jnp.where(first, own, pr[step, EAST, j])
            else:
                win = jnp.where(first, pr[step, WEST, j], own)
            d = (pltpu.roll(win, NL - 1, 1) - win) * eo[side, j]
            before = pltpu.roll(d, 1, 1)
            h = limiter(0.25 * (d + before), before, d)
            g = es[side, j] * win + eb[side, j] * d + ec[side, j] * h + ed[side, j] * pltpu.roll(h, NL - 1, 1)
            sums.append(pltpu.roll(g, 1, 1) - g)
        cc[j] = jnp.where(first, sums[EAST], sums[WEST])

    def edges(step, part):
        for copy in col_copies(step, part):
            copy.wait_recv()
        first, size = ((2, 8), (10, 6), (0, 2))[part]
        for j in range(first, first + size):
            edge_correction(step, j)

    def zonal(q, j):
        correction = cc[j]
        for k in range(NK):
            o, s, b, e = ox[k, j], sx[k, j], bx[k, j], ex[k, j]
            up = s > 0
            for t in range(2):
                x = q[t, k, j + 2]
                d = (pltpu.roll(x, NL - 1, 1) - x) * o
                before = pltpu.roll(d, 1, 1)
                h = limiter(0.25 * (d + before), before, d)
                f = s * x + b * d + e * jnp.where(up, h, pltpu.roll(h, NL - 1, 1))
                n = NK * t + k
                fix = jnp.where(edge_lanes, pltpu.roll(correction, (NL - 2 - 4 * n) % NL, 1), 0.0)
                ax[t, k] = pltpu.roll(f, 1, 1) - f + fix

    def meridional_start(q, j):
        @pl.loop(0, NK // 4)
        def _(kk):
            for k4 in range(4):
                k = 4 * kk + k4
                s, b, e = sy[k, j], by[k, j], ey[k, j]
                for t in range(2):
                    a2, a1, c0, c1 = (q[t, k, j + n] for n in range(4))
                    d2 = (a1 - a2) * oy[k, j]
                    d1 = (c0 - a1) * oy[k, j + 1]
                    d0 = (c1 - c0) * oy[k, j + 2]
                    h1 = limiter(c0 - a2, d2, d1)
                    h0 = limiter(c1 - a1, d1, d0)
                    dy[t, k] = d0
                    hy[t, k] = h0
                    fy[t, k] = s * a1 + b * d1 + e * jnp.where(s > 0, h1, h0)

    def rest(q, out, off, j, step):
        fl = flb[j + 2]
        packed = jnp.zeros((NS, NL), F32)
        state = []
        for t in range(2):
            x0, x1 = q[t, 0, j + 2], q[t, 1, j + 2]
            d0 = (x1 - x0) * oz[0, j]
            state.append([x0, x1, d0, None, None])
        for k in range(NK):
            s, b, e = sy[k, j + 1], by[k, j + 1], ey[k, j + 1]
            up = s > 0
            oy1 = oy[k, j + 3]
            if k < NK - 1:
                zs, ze = sz[k, j], ez[k, j]
                zup = zs > 0
            if k < NK - 2:
                zo = oz[k + 1, j]
            wet = fl > k
            for t in range(2):
                x, below, zd, zh, zf = state[t]
                y1, y2 = q[t, k, j + 3], q[t, k, j + 4]
                d0, h0 = dy[t, k], hy[t, k]
                d1 = (y2 - y1) * oy1
                h1 = limiter(y2 - x, d0, d1)
                f = s * x + b * d0 + e * jnp.where(up, h0, h1)
                acc = (ax[t, k] + fy[t, k]) - f
                dy[t, k] = d1
                hy[t, k] = h1
                fy[t, k] = f
                if k < NK - 1:
                    if k < NK - 2:
                        deeper = q[t, k + 2, j + 2]
                        zd1 = (deeper - below) * zo
                        zh1 = limiter(deeper - x, zd, zd1)
                    else:
                        deeper, zd1, zh1 = None, None, None
                    slope_near = 0.0 if zh is None else zh
                    slope_far = 0.0 if zh1 is None else zh1
                    nf = zs * jnp.where(zup, x, below) + ze * jnp.where(zup, slope_near, slope_far)
                    acc = acc - nf
                    state[t] = [below, deeper, zd1, zh1, nf]
                if zf is not None:
                    acc = acc + zf
                if step == 0:
                    new = jnp.where(wet, x, 0.0) + acc
                else:
                    new = x + acc
                out[t, k, j + off] = new
                if step == 0:
                    n = NK * t + k
                    moved = pltpu.roll(jnp.where(edge_lanes, new, 0.0), (4 * n + 2) % NL, 1)
                    packed = packed + moved
        if step == 0:
            pq[1, j] = packed

    def sweep(q, out, off, step, at_edge_b, at_rows, at_half):
        zonal(q, 2)
        meridional_start(q, 2)

        @pl.loop(0, NJ)
        def _(i):
            j = (i + 2) & (NJ - 1)

            @pl.when(i == 7)
            def _():
                at_edge_b()

            @pl.when(i == 8)
            def _():
                at_half()

            @pl.when(i == 12)
            def _():
                at_rows()

            @pl.when(i == 14)
            def _():
                meridional_start(q, 0)

            rest(q, out, off, j, step)
            zonal(q, (j + 1) & (NJ - 1))

    def nothing():
        pass

    def send_half():
        for copy in col_copies(1, 0):
            copy.start()

    for part in range(3):
        edges(0, part)
    sweep(q0, q1, 2, 0, nothing, nothing, send_half)
    for part in (1, 2):
        for copy in col_copies(1, part):
            copy.start()

    def row2_north(slot):
        return remote(
            q1.at[:, :, pl.ds(NJ, 2), NS - 1, :], hq.at[1, slot, :, :, :, 0, :],
            row2_send.at[0], row2_recv.at[slot], north,
        )

    def row2_south():
        return remote(
            q1.at[:, :, pl.ds(2, 2), 0, :], hq.at[1, NORTH, :, :, :, 0, :],
            row2_send.at[1], row2_recv.at[NORTH], south,
        )

    row2_north(nslot).start()

    @pl.when(low)
    def _():
        row2_south().start()

    def at_edge_b():
        edges(1, 1)
        edges(1, 2)

    def at_rows():
        row2_north(NORTH).wait_recv()

        @pl.when(low)
        def _():
            row2_north(SOUTH).wait_recv()

        halo_q(1, q1)

    def out_copies(part):
        first, size = ((2, 8), (10, 6), (0, 2))[part]
        return [
            pltpu.make_async_copy(
                ob.at[t, :, pl.ds(first, size), s, :],
                dst.at[:, pl.ds(NJ * s + first, size), :],
                out_sem.at[t, s, part],
            )
            for t, dst in enumerate((tout_hbm, sout_hbm))
            for s in range(NS)
        ]

    def out_half():
        for copy in out_copies(0):
            copy.start()

    edges(1, 0)
    sweep(q1, ob, 0, 1, at_edge_b, at_rows, out_half)
    for part in (1, 2):
        for copy in out_copies(part):
            copy.start()

    for copy in north_rows(nslot):
        copy.wait_send()
    row2_north(nslot).wait_send()

    @pl.when(low)
    def _():
        for copy in south_rows():
            copy.wait_send()
        row2_south().wait_send()

    for copy in static_col_copies():
        copy.wait_send()
    for step in range(2):
        for part in range(3):
            for copy in col_copies(step, part):
                copy.wait_send()
    for part in range(3):
        for copy in out_copies(part):
            copy.wait()


def on_device(t, s, u, v, w, kap, sea, bot):
    def vm(*lead):
        return pltpu.VMEM(lead + (NS, NL), F32)

    def vi(*lead):
        return pltpu.VMEM(lead + (NS, NL), jnp.int32)

    dma = pltpu.SemaphoreType.DMA
    anywhere = pl.BlockSpec(memory_space=pl.ANY)
    shape = jax.ShapeDtypeStruct(t.shape, F32)
    return pl.pallas_call(
        kernel,
        out_shape=(shape, shape),
        in_specs=[anywhere] * 8,
        out_specs=(anywhere, anywhere),
        scratch_shapes=[
            vm(2, NK, NJ + 4), vm(2, NK, NJ + 4), vm(2, NK, NJ),
            vm(NK, NJ), vm(NK, NJ), vm(NK, NJ + 1), vm(NK, NJ + 2),
            vi(NJ + 4), vi(NJ + 4), vm(NJ + 4),
            vm(NK, NJ), vm(NK, NJ), vm(NK, NJ), vm(NK, NJ),
            vm(NK, NJ + 3), vm(NK, NJ + 1), vm(NK, NJ + 1), vm(NK, NJ + 1),
            vm(NK, NJ), vm(NK, NJ), vm(NK, NJ),
            vm(2, NK), vm(2, NK), vm(2, NK), vm(2, NK),
            vm(2, 2, 2, NK, 2), vm(2, NK, 1), vm(2, NK, 1), vi(2, 2), vi(2, 2),
            vm(2, NJ), vm(2, 2, NJ), vm(NJ), vm(2, NJ), vm(), vm(2), vm(NJ),
            vm(2, NJ), vm(2, NJ), vm(2, NJ), vm(2, NJ), vm(2, NJ),
            dma((8,)), dma((2, NS, 3)), dma((2, 6)), dma((2, 6)), dma((2,)), dma((2,)),
            dma((2, 2)), dma((2, 2)), dma((2, 2, 3)), dma((2, 2, 3)),
        ],
        compiler_params=pltpu.CompilerParams(
            collective_id=0, has_side_effects=True, vmem_limit_bytes=50 * 1024 * 1024
        ),
        cost_estimate=pl.CostEstimate(flops=120_000_000, bytes_accessed=9_000_000, transcendentals=0),
    )(t, s, u, v, w, kap, sea, bot)


def solution(mesh):
    block = P(None, "ja", "ia")
    flat = P("ja", "ia")
    return jax.shard_map(
        on_device,
        mesh=mesh,
        in_specs=(block,) * 6 + (flat, flat),
        out_specs=(block, block),
        check_vma=False,
    )
```

profile of v0, /device:TPU:26, one launch (start us, length us, event | category | flops | bytes accessed | tf_op | source)
XLA Modules:
  0.0 42.1 jit_solution(8718301077385541279)
XLA Ops:
  0.6 0.0 copy-start
  0.6 1.2 %copy-done = f32[16,128,128]{2,1,0:T(8,128)S(1)} copy-done((f32[16,128,128]{2,1,0:T(8,128)S(1)}, f32[16,128,128]{2,1,0:T(8,128)}, u32[]{:S(2)}) %copy-start) | copy-done | bytes 1048600
  1.9 0.0 copy-start.1
  1.9 0.8 %copy-done.1 = s32[128,128]{1,0:T(8,128)S(1)} copy-done((s32[128,128]{1,0:T(8,128)S(1)}, s32[128,128]{1,0:T(8,128)}, u32[]{:S(2)}) %copy-start.1) | copy-done | bytes 65560
  2.7 0.0 copy-start.2
  2.7 0.8 %copy-done.2 = s32[128,128]{1,0:T(8,128)S(1)} copy-done((s32[128,128]{1,0:T(8,128)S(1)}, s32[128,128]{1,0:T(8,128)}, u32[]{:S(2)}) %copy-start.2) | copy-done | bytes 65560
  3.5 36.6 %shard_map.95 = (f32[16,128,128]{2,1,0:T(8,128)S(1)}, f32[16,128,128]{2,1,0:T(8,128)S(1)}) custom-call(f32[16,128,128]{2,1,0:T(8,128)S(1)} %copy-done, f32[16,128,128]{2,1,0:T(8,128)} %s_hbm.1, f32[16,128,128]{2,1,0:T(8,128)} %u_hbm.1, f32[16,128,128]{2,1,0:T(8,128)} %v_hbm.1, f32[16,128,128]{2,1,0:T(8,128)} %w_hbm.1, f32[16,128,128]{2,1,0:T(8,128)} %k_hbm.1, ...), custom_call_target="tpu_custom_call" | custom-call | flops 120000000 | bytes 9000000 | tf_op jit(solution)/shard_map/pallas_call | solution.py:577
  40.1 1.0 %copy.12 = f32[16,128,128]{2,1,0:T(8,128)} copy(f32[16,128,128]{2,1,0:T(8,128)S(1)} %get-tuple-element.4) | data formatting | bytes 2097152
  41.1 1.0 %copy.13 = f32[16,128,128]{2,1,0:T(8,128)} copy(f32[16,128,128]{2,1,0:T(8,128)S(1)} %get-tuple-element.5) | data formatting | bytes 2097152
Async XLA Ops:
  0.6 1.2 %copy-start = (f32[16,128,128]{2,1,0:T(8,128)S(1)}, f32[16,128,128]{2,1,0:T(8,128)}, u32[]{:S(2)}) copy-start(f32[16,128,128]{2,1,0:T(8,128)} %t_hbm.1) | copy-start | bytes 3145732
  1.9 0.8 %copy-start.1 = (s32[128,128]{1,0:T(8,128)S(1)}, s32[128,128]{1,0:T(8,128)}, u32[]{:S(2)}) copy-start(s32[128,128]{1,0:T(8,128)} %sea_hbm.1) | copy-start | bytes 196612
  2.7 0.8 %copy-start.2 = (s32[128,128]{1,0:T(8,128)S(1)}, s32[128,128]{1,0:T(8,128)}, u32[]{:S(2)}) copy-start(s32[128,128]{1,0:T(8,128)} %bot_hbm.1) | copy-start | bytes 196612
where the time goes:
time: 42.3 us; the launch traced here: 42.1 us
  Pallas kernels  36.6 us (87%)
  local copies, waits for them, and re-layouts  4.84 us (11%)
  between operations  0.65 us (2%)
    pallas_call x1, Pallas kernels, on_device(): pl.pallas_call(kernel, out_shape=(shape, shape), in_specs=[anywhere] * 8,...  36.6 us
    unnamed x8, local copies, waits for them, and re-layouts  4.84 us

commit v1 on v0

--- a/solution.py
+++ b/solution.py
@@ -30,7 +30,7 @@
     tout_hbm, sout_hbm,
     q0, q1, ob, ub, wb, vb, kb, seab, botb, flb,
     ox, sx, bx, ex, oy, sy, by, ey, oz, sz, ez,
-    ax, dy, hy, fy,
+    oxw, dx, hx, fx, dy, hy, fy,
     hq, hk, hv, hs, hb,
     pq, pr, uko, ukr, flo, flr, cc,
     eo, es, eb, ec, ed,
@@ -197,11 +197,13 @@
     def _(j):
         fl = flb[j + 2]
         face = jnp.where(lane == NL - 1, 0.0, jnp.minimum(fl, pltpu.roll(fl, NL - 1, 1)))
+        face_w = jnp.where(lane == 0, 0.0, jnp.minimum(fl, pltpu.roll(fl, 1, 1)))
         for k in range(NK):
             is_open = face > k
             u = ub[k, j]
             kap = kb[k, j + 1]
             ox[k, j] = jnp.where(is_open, 4.0, 0.0)
+            oxw[k, j] = jnp.where(face_w > k, 4.0, 0.0)
             sx[k, j] = jnp.where(is_open, u, 0.0)
             bx[k, j] = jnp.minimum(0.25 * u, 0.0) - 0.125 * (kap + pltpu.roll(kap, NL - 1, 1))
             ex[k, j] = quarter_edge(u)
@@ -233,14 +235,11 @@
         @pl.when(top)
         def _():
             for t in range(2):
-                @pl.loop(0, NK // 4)
-                def _(kk):
-                    for k4 in range(4):
-                        k = 4 * kk + k4
-                        near = mirror(hq[step, NORTH, t, k, 1])
-                        far = mirror(hq[step, NORTH, t, k, 0])
-                        hq[step, NORTH, t, k, 0] = near
-                        hq[step, NORTH, t, k, 1] = far
+                for k in range(NK):
+                    near = mirror(hq[step, NORTH, t, k, 1])
+                    far = mirror(hq[step, NORTH, t, k, 0])
+                    hq[step, NORTH, t, k, 0] = near
+                    hq[step, NORTH, t, k, 1] = far
 
     def halo_q(step, q):
         fold_q(step)
@@ -362,20 +361,36 @@
         for j in range(first, first + size):
             edge_correction(step, j)
 
-    def zonal(q, j):
-        correction = cc[j]
+    def zonal_slopes(q, j, slot):
         for k in range(NK):
-            o, s, b, e = ox[k, j], sx[k, j], bx[k, j], ex[k, j]
+            o, ow = ox[k, j], oxw[k, j]
+            for t in range(2):
+                x = q[t, k, j + 2]
+                after = pltpu.roll(x, NL - 1, 1)
+                before = pltpu.roll(x, 1, 1)
+                d = (after - x) * o
+                dx[slot, t, k] = d
+                hx[slot, t, k] = limiter(after - before, (x - before) * ow, d)
+
+    def zonal_fluxes(q, j, slot):
+        for k in range(NK):
+            s, b, e = sx[k, j], bx[k, j], ex[k, j]
             up = s > 0
             for t in range(2):
-                x = q[t, k, j + 2]
-                d = (pltpu.roll(x, NL - 1, 1) - x) * o
-                before = pltpu.roll(d, 1, 1)
-                h = limiter(0.25 * (d + before), before, d)
-                f = s * x + b * d + e * jnp.where(up, h, pltpu.roll(h, NL - 1, 1))
+                x, d, h = q[t, k, j + 2], dx[slot, t, k], hx[slot, t, k]
+                fx[slot, t, k] = s * x + b * d + e * jnp.where(up, h, pltpu.roll(h, NL - 1, 1))
+
+    def repack(out, off, j):
+        sums = []
+        for t in range(2):
+            for k in range(NK):
                 n = NK * t + k
-                fix = jnp.where(edge_lanes, pltpu.roll(correction, (NL - 2 - 4 * n) % NL, 1), 0.0)
-                ax[t, k] = pltpu.roll(f, 1, 1) - f + fix
+                moved = pltpu.roll(jnp.where(edge_lanes, out[t, k, j + off], 0.0), (4 * n + 2) % NL, 1)
+                if len(sums) < 4:
+                    sums.append(moved)
+                else:
+                    sums[n % 4] = sums[n % 4] + moved
+        pq[1, j] = (sums[0] + sums[1]) + (sums[2] + sums[3])
 
     def meridional_start(q, j):
         @pl.loop(0, NK // 4)
@@ -394,9 +409,9 @@
                     hy[t, k] = h0
                     fy[t, k] = s * a1 + b * d1 + e * jnp.where(s > 0, h1, h0)
 
-    def rest(q, out, off, j, step):
+    def rest(q, out, off, j, step, slot):
         fl = flb[j + 2]
-        packed = jnp.zeros((NS, NL), F32)
+        correction = cc[j]
         state = []
         for t in range(2):
             x0, x1 = q[t, 0, j + 2], q[t, 1, j + 2]
@@ -419,7 +434,10 @@
                 d1 = (y2 - y1) * oy1
                 h1 = limiter(y2 - x, d0, d1)
                 f = s * x + b * d0 + e * jnp.where(up, h0, h1)
-                acc = (ax[t, k] + fy[t, k]) - f
+                n = NK * t + k
+                flux = fx[slot, t, k]
+                fix = jnp.where(edge_lanes, pltpu.roll(correction, (NL - 2 - 4 * n) % NL, 1), 0.0)
+                acc = ((pltpu.roll(flux, 1, 1) - flux) + (fy[t, k] - f)) + fix
                 dy[t, k] = d1
                 hy[t, k] = h1
                 fy[t, k] = f
@@ -442,39 +460,41 @@
                 else:
                     new = x + acc
                 out[t, k, j + off] = new
-                if step == 0:
-                    n = NK * t + k
-                    moved = pltpu.roll(jnp.where(edge_lanes, new, 0.0), (4 * n + 2) % NL, 1)
-                    packed = packed + moved
-        if step == 0:
-            pq[1, j] = packed
 
     def sweep(q, out, off, step, at_edge_b, at_rows, at_half):
-        zonal(q, 2)
+        zonal_slopes(q, 2, 0)
+        zonal_slopes(q, 3, 1)
+        zonal_fluxes(q, 2, 0)
         meridional_start(q, 2)
 
-        @pl.loop(0, NJ)
+        @pl.loop(0, NJ // 2)
         def _(i):
-            j = (i + 2) & (NJ - 1)
+            @pl.when(i == 4)
+            def _():
+                at_edge_b()
+
+            @pl.when(i == 5)
+            def _():
+                at_half()
+
+            @pl.when(i == 6)
+            def _():
+                at_rows()
 
             @pl.when(i == 7)
             def _():
-                at_edge_b()
-
-            @pl.when(i == 8)
-            def _():
-                at_half()
-
-            @pl.when(i == 12)
-            def _():
-                at_rows()
-
-            @pl.when(i == 14)
-            def _():
                 meridional_start(q, 0)
 
-            rest(q, out, off, j, step)
-            zonal(q, (j + 1) & (NJ - 1))
+            for half in range(2):
+                j = (2 * i + 2 + half) & (NJ - 1)
+                if step == 0:
+                    repack(out, off, (j - 1) & (NJ - 1))
+                rest(q, out, off, j, step, half)
+                zonal_fluxes(q, (j + 1) & (NJ - 1), 1 - half)
+                zonal_slopes(q, (j + 2) & (NJ - 1), half)
+
+        if step == 0:
+            repack(out, off, 1)
 
     def nothing():
         pass
@@ -586,7 +606,7 @@
             vm(NK, NJ), vm(NK, NJ), vm(NK, NJ), vm(NK, NJ),
             vm(NK, NJ + 3), vm(NK, NJ + 1), vm(NK, NJ + 1), vm(NK, NJ + 1),
             vm(NK, NJ), vm(NK, NJ), vm(NK, NJ),
-            vm(2, NK), vm(2, NK), vm(2, NK), vm(2, NK),
+            vm(NK, NJ), vm(2, 2, NK), vm(2, 2, NK), vm(2, 2, NK), vm(2, NK), vm(2, NK), vm(2, NK),
             vm(2, 2, 2, NK, 2), vm(2, NK, 1), vm(2, NK, 1), vi(2, 2), vi(2, 2),
             vm(2, NJ), vm(2, 2, NJ), vm(NJ), vm(2, NJ), vm(), vm(2), vm(NJ),
             vm(2, NJ), vm(2, NJ), vm(2, NJ), vm(2, NJ), vm(2, NJ),
@@ -594,7 +614,7 @@
             dma((2, 2)), dma((2, 2)), dma((2, 2, 3)), dma((2, 2, 3)),
         ],
         compiler_params=pltpu.CompilerParams(
-            collective_id=0, has_side_effects=True, vmem_limit_bytes=50 * 1024 * 1024
+            collective_id=0, has_side_effects=True, vmem_limit_bytes=58 * 1024 * 1024
         ),
         cost_estimate=pl.CostEstimate(flops=120_000_000, bytes_accessed=9_000_000, transcendentals=0),
     )(t, s, u, v, w, kap, sea, bot)

time: 42.3 us -> 35.7 us (0.84)
  Pallas kernels: 36.6 us -> 31.6 us
  local copies, waits for them, and re-layouts: 4.84 us -> 3.36 us
    pallas_call x1, Pallas kernels: 36.6 us -> 31.6 us  [on_device(): pl.pallas_call(kernel, out_shape=(shape, shape), in_specs=[anywhere] * 8,...]
    unnamed x8 -> x4, local copies, waits for them, and re-layouts: 4.84 us -> 3.36 us
where the time goes in v1:
time: 35.7 us; the launch traced here: 35.6 us
  Pallas kernels  31.6 us (89%)
  local copies, waits for them, and re-layouts  3.36 us (9%)
  between operations  0.65 us (2%)
    pallas_call x1, Pallas kernels, on_device(): pl.pallas_call(kernel, out_shape=(shape, shape), in_specs=[anywhere] * 8,...  31.6 us
    unnamed x4, local copies, waits for them, and re-layouts  3.36 us

profile of v1, /device:TPU:26, one launch (start us, length us, event | category | flops | bytes accessed | tf_op | source)
XLA Modules:
  0.0 35.6 jit_solution(5194162259532860970)
XLA Ops:
  0.6 31.6 %shard_map.95 = (f32[16,128,128]{2,1,0:T(8,128)}, f32[16,128,128]{2,1,0:T(8,128)}) custom-call(f32[16,128,128]{2,1,0:T(8,128)} %t_hbm.1, f32[16,128,128]{2,1,0:T(8,128)} %s_hbm.1, f32[16,128,128]{2,1,0:T(8,128)} %u_hbm.1, f32[16,128,128]{2,1,0:T(8,128)} %v_hbm.1, f32[16,128,128]{2,1,0:T(8,128)} %w_hbm.1, f32[16,128,128]{2,1,0:T(8,128)} %k_hbm.1, ...), custom_call_target="tpu_custom_call" | custom-call | flops 120000000 | bytes 9000000 | tf_op jit(solution)/shard_map/pallas_call | solution.py:597
  32.2 0.0 copy-start
  32.2 2.4 %copy.12 = f32[16,128,128]{2,1,0:T(8,128)} copy(f32[16,128,128]{2,1,0:T(8,128)} %get-tuple-element.4) | data formatting | bytes 2097152
  34.6 0.0 copy-done
  34.6 1.0 %copy.13 = f32[16,128,128]{2,1,0:T(8,128)} copy(f32[16,128,128]{2,1,0:T(8,128)S(1)} %copy-done) | data formatting | bytes 2097152
Async XLA Ops:
  32.2 2.4 %copy-start = (f32[16,128,128]{2,1,0:T(8,128)S(1)}, f32[16,128,128]{2,1,0:T(8,128)}, u32[]{:S(2)}) copy-start(f32[16,128,128]{2,1,0:T(8,128)} %get-tuple-element.5) | copy-start | bytes 3145732

commit v2 on v1

--- a/solution.py
+++ b/solution.py
@@ -31,10 +31,10 @@
     q0, q1, ob, ub, wb, vb, kb, seab, botb, flb,
     ox, sx, bx, ex, oy, sy, by, ey, oz, sz, ez,
     oxw, dx, hx, fx, dy, hy, fy,
-    hq, hk, hv, hs, hb,
+    rown, rhal, rk, rkh, rv, rvh, hs, hb, rcoef, rc,
     pq, pr, uko, ukr, flo, flr, cc,
     eo, es, eb, ec, ed,
-    in_sem, out_sem, row_send, row_recv, row2_send, row2_recv,
+    in_sem, own_sem, own2_sem, out_sem, row_send, row_recv, row2_send, row2_recv,
     col_send, col_recv, col2_send, col2_recv,
 ):
     ia = lax.axis_index("ia")
@@ -84,7 +84,21 @@
     def loaded(index, whole):
         pltpu.make_async_copy(whole, whole, in_sem.at[index]).wait()
 
-    pl.semaphore_wait(barrier, jnp.where(low, 4, 3))
+    rows_total = NJ * NS
+    edge_rows = (0, 1, rows_total - 2, rows_total - 1)
+
+    def own_row_copies():
+        pairs = [
+            (src.at[:, row, :], rown.at[0, t, a])
+            for t, src in enumerate((t_hbm, s_hbm))
+            for a, row in enumerate(edge_rows)
+        ]
+        pairs += [(k_hbm.at[:, row, :], rk.at[a]) for a, row in enumerate((0, rows_total - 1))]
+        pairs += [(v_hbm.at[:, row, :], rv.at[a]) for a, row in enumerate((0, rows_total - 2, rows_total - 1))]
+        return [pltpu.make_async_copy(a, b, own_sem.at[n]) for n, (a, b) in enumerate(pairs)]
+
+    for copy in own_row_copies():
+        copy.start()
 
     def remote(src, dst, ssem, rsem, device):
         return pltpu.make_async_remote_copy(
@@ -94,35 +108,26 @@
 
     def row_copies(first, last, slot, direction, device):
         pair = pl.ds(first, 2)
-        line = pl.ds(last, 1)
         parts = [
-            (t_hbm.at[:, pair, :], hq.at[0, slot, 0, :, :, 0, :]),
-            (s_hbm.at[:, pair, :], hq.at[0, slot, 1, :, :, 0, :]),
-            (k_hbm.at[:, line, :], hk.at[slot, :, :, 0, :]),
-            (v_hbm.at[:, line, :], hv.at[slot, :, :, 0, :]),
-            (sea_hbm.at[pair, :], hs.at[slot, :, 0, :]),
-            (bot_hbm.at[pair, :], hb.at[slot, :, 0, :]),
+            (src.at[:, first + r, :], rhal.at[0, slot, t, r])
+            for t, src in enumerate((t_hbm, s_hbm))
+            for r in range(2)
+        ] + [
+            (k_hbm.at[:, last, :], rkh.at[slot]),
+            (v_hbm.at[:, last, :], rvh.at[slot]),
+            (sea_hbm.at[pair, :], hs.at[slot]),
+            (bot_hbm.at[pair, :], hb.at[slot]),
         ]
         return [
             remote(src, dst, row_send.at[direction, n], row_recv.at[slot, n], device)
             for n, (src, dst) in enumerate(parts)
         ]
 
-    rows_total = NJ * NS
-
     def north_rows(slot):
         return row_copies(rows_total - 2, rows_total - 1, slot, 0, north)
 
     def south_rows():
         return row_copies(0, 0, NORTH, 1, south)
-
-    for copy in north_rows(nslot):
-        copy.start()
-
-    @pl.when(low)
-    def _():
-        for copy in south_rows():
-            copy.start()
 
     def pack(load_vreg, count):
         acc = jnp.zeros((NS, NL), F32)
@@ -131,8 +136,10 @@
             acc = jnp.where(group == n, moved, acc)
         return acc
 
+    PARTS = ((0, NJ),), ((2, NJ - 4), (NJ - 2, 2), (0, 2))
+
     def col_copies(step, part):
-        first, size = ((2, 8), (10, 6), (0, 2))[part]
+        first, size = PARTS[step][part]
         sl = pl.ds(first, size)
         return [
             remote(pq.at[step, sl], pr.at[step, EAST, sl], col2_send.at[step, 0, part], col2_recv.at[step, EAST, part], west),
@@ -150,15 +157,11 @@
     loaded(0, q0.at[0, :, pl.ds(2, NJ)])
     loaded(1, q0.at[1, :, pl.ds(2, NJ)])
 
-    @pl.loop(0, NJ // 2)
-    def _(half):
-        for h in range(2):
-            j = 2 * half + h
+    @pl.loop(0, NJ // 4)
+    def _(quarter):
+        for h in range(4):
+            j = 4 * quarter + h
             pq[0, j] = pack(lambda n: q0[n // NK, n % NK, j + 2], 2 * NK)
-
-    for part in range(3):
-        for copy in col_copies(0, part):
-            copy.start()
 
     loaded(2, seab.at[pl.ds(2, NJ)])
     loaded(3, botb.at[pl.ds(2, NJ)])
@@ -168,14 +171,26 @@
     loaded(4, ub)
     loaded(5, kb.at[:, pl.ds(1, NJ)])
 
-    @pl.loop(0, NJ // 2)
-    def _(half):
-        for h in range(2):
-            j = 2 * half + h
+    @pl.loop(0, NJ // 4)
+    def _(quarter):
+        for h in range(4):
+            j = 4 * quarter + h
             uko[j] = pack(lambda n: ub[n, j] if n < NK else kb[n - NK, j + 1], 2 * NK)
 
-    for copy in static_col_copies():
-        copy.start()
+    def first_sends():
+        pl.semaphore_wait(barrier, jnp.where(low, 4, 3))
+        for copy in col_copies(0, 0):
+            copy.start()
+        for copy in north_rows(nslot):
+            copy.start()
+
+        @pl.when(low)
+        def _():
+            for copy in south_rows():
+                copy.start()
+
+        for copy in static_col_copies():
+            copy.start()
 
     loaded(6, vb.at[:, pl.ds(1, NJ)])
     loaded(7, wb)
@@ -219,86 +234,134 @@
         open_y(j)
         coef_y(j)
 
-    south_sub = (sub == 0) & low
-    north_sub = sub == 0
-
-    def mirror(x):
-        return jnp.take_along_axis(x, NL - 1 - lane, axis=1)
-
-    def from_south(halo, own):
-        return jnp.where(south_sub, halo, pltpu.roll(own, 1, 0))
-
-    def from_north(halo, own):
-        return pltpu.roll(jnp.where(north_sub, halo, own), NS - 1, 0)
-
-    def fold_q(step):
-        @pl.when(top)
-        def _():
-            for t in range(2):
-                for k in range(NK):
-                    near = mirror(hq[step, NORTH, t, k, 1])
-                    far = mirror(hq[step, NORTH, t, k, 0])
-                    hq[step, NORTH, t, k, 0] = near
-                    hq[step, NORTH, t, k, 1] = far
-
-    def halo_q(step, q):
-        fold_q(step)
-
-        @pl.loop(0, NK // 4)
-        def _(kk):
-            for k4 in range(4):
-                k = 4 * kk + k4
-                for t in range(2):
-                    for r in range(2):
-                        q[t, k, r] = from_south(hq[step, SOUTH, t, k, r], q[t, k, NJ + r])
-                        q[t, k, NJ + 2 + r] = from_north(hq[step, NORTH, t, k, r], q[t, k, 2 + r])
-
-    def wait_rows(slot):
-        for copy in (row_copies(0, 0, slot, 0, north)):
-            copy.wait_recv()
-
-    wait_rows(NORTH)
-
-    @pl.when(low)
-    def _():
-        wait_rows(SOUTH)
-
-    @pl.when(top)
-    def _():
-        for k in range(NK):
-            hk[NORTH, k, 0] = mirror(hk[NORTH, k, 0])
-        for h in (hs, hb):
-            near = mirror(h[NORTH, 1])
-            far = mirror(h[NORTH, 0])
-            h[NORTH, 0] = near
-            h[NORTH, 1] = far
-
     for r in range(2):
-        south_floor = (hs[SOUTH, r] * hb[SOUTH, r]).astype(F32)
-        north_floor = (hs[NORTH, r] * hb[NORTH, r]).astype(F32)
-        flb[r] = jnp.where(
-            sub == 0, jnp.where(low, south_floor, 0.0), pltpu.roll(flb[NJ + r], 1, 0)
-        )
-        flb[NJ + 2 + r] = from_north(north_floor, flb[2 + r])
+        flb[r] = jnp.where(sub == 0, 0.0, pltpu.roll(flb[NJ + r], 1, 0))
+        flb[NJ + 2 + r] = jnp.where(sub == NS - 1, 0.0, pltpu.roll(flb[2 + r], NS - 1, 0))
     for k in range(NK):
-        kb[k, 0] = from_south(hk[SOUTH, k, 0], kb[k, NJ])
-        kb[k, NJ + 1] = from_north(hk[NORTH, k, 0], kb[k, 1])
-        vb[k, 0] = from_south(hv[SOUTH, k, 0], vb[k, NJ])
+        kb[k, 0] = pltpu.roll(kb[k, NJ], 1, 0)
+        kb[k, NJ + 1] = pltpu.roll(kb[k, 1], NS - 1, 0)
+        vb[k, 0] = pltpu.roll(vb[k, NJ], 1, 0)
     for j in (-2, -1, NJ - 1, NJ):
         open_y(j)
     for j in (-1, NJ - 1):
         coef_y(j)
-    halo_q(0, q0)
-
-    for copy in static_col_copies():
-        copy.wait_recv()
+
+    def wrap_rows(q):
+        for t in range(2):
+            for k in range(NK):
+                for r in range(2):
+                    q[t, k, r] = pltpu.roll(q[t, k, NJ + r], 1, 0)
+                    q[t, k, NJ + 2 + r] = pltpu.roll(q[t, k, 2 + r], NS - 1, 0)
+
+    wrap_rows(q0)
+    first_sends()
+
+    def mirror(x):
+        return jnp.take_along_axis(x, NL - 1 - lane, axis=1)
+
+    def levels(kk):
+        return pl.ds(NS * kk, NS)
+
+    def fold(step):
+        @pl.when(top)
+        def _():
+            for t in range(2):
+                for kk in range(NK // NS):
+                    lv = levels(kk)
+                    near = mirror(rhal[step, NORTH, t, 1, lv, :])
+                    far = mirror(rhal[step, NORTH, t, 0, lv, :])
+                    rhal[step, NORTH, t, 0, lv, :] = near
+                    rhal[step, NORTH, t, 1, lv, :] = far
+            if step == 0:
+                for kk in range(NK // NS):
+                    rkh[NORTH, levels(kk), :] = mirror(rkh[NORTH, levels(kk), :])
+                for h in (hs, hb):
+                    near = mirror(jnp.broadcast_to(h[NORTH, 1:2, :], (NS, NL)))
+                    far = mirror(jnp.broadcast_to(h[NORTH, 0:1, :], (NS, NL)))
+                    h[NORTH, 0:1, :] = near[0:1]
+                    h[NORTH, 1:2, :] = far[0:1]
+
+    def row_static():
+        def line(x):
+            return jnp.broadcast_to(x, (NS, NL))
+
+        def halo_floor(slot, r):
+            return line((hs[slot, r : r + 1, :] * hb[slot, r : r + 1, :]).astype(F32))
+
+        south_floors = [
+            jnp.where(low, halo_floor(SOUTH, 0), 0.0),
+            jnp.where(low, halo_floor(SOUTH, 1), 0.0),
+            line(flb[2, 0:1, :]),
+            line(flb[3, 0:1, :]),
+        ]
+        north_floors = [
+            line(flb[NJ, NS - 1 : NS, :]),
+            line(flb[NJ + 1, NS - 1 : NS, :]),
+            halo_floor(NORTH, 0),
+            halo_floor(NORTH, 1),
+        ]
+        for kk in range(NK // NS):
+            lv = levels(kk)
+            depth = (sub + NS * kk).astype(F32)
+            for side, floors in ((SOUTH, south_floors), (NORTH, north_floors)):
+                if side == SOUTH:
+                    v = jnp.where(low, rvh[SOUTH, lv, :], 0.0)
+                    ka, kc = jnp.where(low, rkh[SOUTH, lv, :], 0.0), rk[0, lv, :]
+                    inner = rv[0, lv, :]
+                    keep = inner > 0
+                else:
+                    v = rv[2, lv, :]
+                    ka, kc = rk[1, lv, :], rkh[NORTH, lv, :]
+                    inner = rv[1, lv, :]
+                    keep = inner <= 0
+                for n in range(3):
+                    is_open = jnp.minimum(floors[n], floors[n + 1]) > depth
+                    rcoef[side, n, lv, :] = jnp.where(is_open, 4.0, 0.0)
+                    if n == 1:
+                        rcoef[side, 3, lv, :] = jnp.where(is_open, v, 0.0)
+                rcoef[side, 4, lv, :] = jnp.minimum(0.25 * v, 0.0) - 0.125 * (ka + kc)
+                rcoef[side, 5, lv, :] = quarter_edge(v)
+                rcoef[side, 6, lv, :] = jnp.where(keep, quarter_edge(inner), 0.0)
+
+    def row_correction(step):
+        for t in range(2):
+            for kk in range(NK // NS):
+                lv = levels(kk)
+                for side in (SOUTH, NORTH):
+                    own = [rown[step, t, 2 * side + r, lv, :] for r in range(2)]
+                    if side == SOUTH:
+                        halo = [jnp.where(low, rhal[step, SOUTH, t, r, lv, :], 0.0) for r in range(2)]
+                        w = halo + own
+                    else:
+                        halo = [rhal[step, NORTH, t, r, lv, :] for r in range(2)]
+                        w = own + halo
+                    d = [(w[n + 1] - w[n]) * rcoef[side, n, lv, :] for n in range(3)]
+                    h1 = limiter(w[2] - w[0], d[0], d[1])
+                    h2 = limiter(w[3] - w[1], d[1], d[2])
+                    s = rcoef[side, 3, lv, :]
+                    f = s * w[1] + rcoef[side, 4, lv, :] * d[1] + rcoef[side, 5, lv, :] * jnp.where(s > 0, h1, h2)
+                    g = rcoef[side, 6, lv, :] * (h2 if side == SOUTH else h1)
+                    if side == SOUTH:
+                        rc[t, 0, lv, :] = f - g
+                        rc[t, 1, lv, :] = g
+                    else:
+                        rc[t, 2, lv, :] = -g
+                        rc[t, 3, lv, :] = g - f
+
+    def add_rows(out, off):
+        for a, (j, s) in enumerate(((0, 0), (1, 0), (NJ - 2, NS - 1), (NJ - 1, NS - 1))):
+            for t in range(2):
+                for k in range(NK):
+                    out[t, k, j + off, s : s + 1, :] = out[t, k, j + off, s : s + 1, :] + rc[t, a, k : k + 1, :]
+
+    def wait_rows(slot):
+        for copy in row_copies(0, 0, slot, 0, north):
+            copy.wait_recv()
 
     level4 = (group & (NK - 1)).astype(F32)
 
-    @pl.loop(0, NJ // 4)
-    def _(quarter):
-        for j4 in range(4):
-            j = 4 * quarter + j4
+    def edge_static():
+        for j in range(NJ):
             index = 4 * j + l4
 
             def spread(x):
@@ -354,12 +417,13 @@
             sums.append(pltpu.roll(g, 1, 1) - g)
         cc[j] = jnp.where(first, sums[EAST], sums[WEST])
 
-    def edges(step, part):
-        for copy in col_copies(step, part):
-            copy.wait_recv()
-        first, size = ((2, 8), (10, 6), (0, 2))[part]
-        for j in range(first, first + size):
-            edge_correction(step, j)
+    def unpacked(j, n):
+        return jnp.where(edge_lanes, pltpu.roll(cc[j], (NL - 2 - 4 * n) % NL, 1), 0.0)
+
+    def add_columns(out, off, j):
+        for t in range(2):
+            for k in range(NK):
+                out[t, k, j + off] = out[t, k, j + off] + unpacked(j, NK * t + k)
 
     def zonal_slopes(q, j, slot):
         for k in range(NK):
@@ -409,9 +473,8 @@
                     hy[t, k] = h0
                     fy[t, k] = s * a1 + b * d1 + e * jnp.where(s > 0, h1, h0)
 
-    def rest(q, out, off, j, step, slot):
+    def rest(q, out, off, j, step, slot, fix):
         fl = flb[j + 2]
-        correction = cc[j]
         state = []
         for t in range(2):
             x0, x1 = q[t, 0, j + 2], q[t, 1, j + 2]
@@ -434,10 +497,10 @@
                 d1 = (y2 - y1) * oy1
                 h1 = limiter(y2 - x, d0, d1)
                 f = s * x + b * d0 + e * jnp.where(up, h0, h1)
-                n = NK * t + k
                 flux = fx[slot, t, k]
-                fix = jnp.where(edge_lanes, pltpu.roll(correction, (NL - 2 - 4 * n) % NL, 1), 0.0)
-                acc = ((pltpu.roll(flux, 1, 1) - flux) + (fy[t, k] - f)) + fix
+                acc = (pltpu.roll(flux, 1, 1) - flux) + (fy[t, k] - f)
+                if fix:
+                    acc = acc + unpacked(j, NK * t + k)
                 dy[t, k] = d1
                 hy[t, k] = h1
                 fy[t, k] = f
@@ -461,88 +524,134 @@
                     new = x + acc
                 out[t, k, j + off] = new
 
-    def sweep(q, out, off, step, at_edge_b, at_rows, at_half):
+    def sweep(q, out, off, step, first, last, repacking, fixing_in, fixing_out, at_start):
+        @pl.loop(first, last)
+        def _(i):
+            at_start(i)
+
+            for half in range(2):
+                j = (2 * i + 2 + half) & (NJ - 1)
+                if repacking:
+                    repack(out, off, (j - 1) & (NJ - 1))
+                rest(q, out, off, j, step, half, fixing_out)
+                zonal_fluxes(q, (j + 1) & (NJ - 1), 1 - half)
+                zonal_slopes(q, (j + 2) & (NJ - 1), half)
+                if fixing_in:
+                    add_columns(q, 2, j + 3)
+                if fixing_out:
+                    add_columns(out, off, (j - NJ // 2) & (NJ - 1))
+
+    def start_sweep(q):
         zonal_slopes(q, 2, 0)
         zonal_slopes(q, 3, 1)
         zonal_fluxes(q, 2, 0)
         meridional_start(q, 2)
 
-        @pl.loop(0, NJ // 2)
-        def _(i):
-            @pl.when(i == 4)
-            def _():
-                at_edge_b()
-
-            @pl.when(i == 5)
-            def _():
-                at_half()
-
-            @pl.when(i == 6)
-            def _():
-                at_rows()
-
+    def restart(q):
+        def at(i):
             @pl.when(i == 7)
             def _():
                 meridional_start(q, 0)
 
-            for half in range(2):
-                j = (2 * i + 2 + half) & (NJ - 1)
-                if step == 0:
-                    repack(out, off, (j - 1) & (NJ - 1))
-                rest(q, out, off, j, step, half)
-                zonal_fluxes(q, (j + 1) & (NJ - 1), 1 - half)
-                zonal_slopes(q, (j + 2) & (NJ - 1), half)
-
-        if step == 0:
-            repack(out, off, 1)
-
-    def nothing():
-        pass
-
-    def send_half():
-        for copy in col_copies(1, 0):
+        return at
+
+    outer = (NJ - 2, NJ - 1, 0, 1)
+    start_sweep(q0)
+    sweep(q0, q1, 2, 0, 0, 8, True, False, False, restart(q0))
+
+    for copy in own_row_copies():
+        copy.wait()
+    wait_rows(NORTH)
+
+    @pl.when(low)
+    def _():
+        wait_rows(SOUTH)
+
+    fold(0)
+    row_static()
+    row_correction(0)
+    for copy in static_col_copies():
+        copy.wait_recv()
+    for copy in col_copies(0, 0):
+        copy.wait_recv()
+    edge_static()
+    for j in range(NJ):
+        edge_correction(0, j)
+    for j in range(2, NJ - 2):
+        pq[1, j] = pq[1, j] + cc[j]
+    for copy in col_copies(1, 0):
+        copy.start()
+    add_rows(q1, 2)
+    for j in outer:
+        add_columns(q1, 2, j)
+
+    def row2_copies(j, s, slot, direction, device):
+        return [
+            remote(
+                q1.at[t, :, j + r + 2, s, :], rhal.at[1, slot, t, r],
+                row2_send.at[direction, t, r], row2_recv.at[slot, t, r], device,
+            )
+            for t in range(2)
+            for r in range(2)
+        ]
+
+    def north2(slot):
+        return row2_copies(NJ - 2, NS - 1, slot, 0, north)
+
+    def south2():
+        return row2_copies(0, 0, NORTH, 1, south)
+
+    def own2_copies():
+        return [
+            pltpu.make_async_copy(q1.at[t, :, j + 2, s, :], rown.at[1, t, a], own2_sem.at[t, a])
+            for t in range(2)
+            for a, (j, s) in enumerate(((0, 0), (1, 0), (NJ - 2, NS - 1), (NJ - 1, NS - 1)))
+        ]
+
+    for copy in north2(nslot):
+        copy.start()
+
+    @pl.when(low)
+    def _():
+        for copy in south2():
             copy.start()
 
-    for part in range(3):
-        edges(0, part)
-    sweep(q0, q1, 2, 0, nothing, nothing, send_half)
+    for copy in own2_copies():
+        copy.start()
+    for j in outer:
+        repack(q1, 2, j)
     for part in (1, 2):
         for copy in col_copies(1, part):
             copy.start()
 
-    def row2_north(slot):
-        return remote(
-            q1.at[:, :, pl.ds(NJ, 2), NS - 1, :], hq.at[1, slot, :, :, :, 0, :],
-            row2_send.at[0], row2_recv.at[slot], north,
-        )
-
-    def row2_south():
-        return remote(
-            q1.at[:, :, pl.ds(2, 2), 0, :], hq.at[1, NORTH, :, :, :, 0, :],
-            row2_send.at[1], row2_recv.at[NORTH], south,
-        )
-
-    row2_north(nslot).start()
+    for j in (2, 3, 4, NJ - 3):
+        add_columns(q1, 2, j)
+    wrap_rows(q1)
+    start_sweep(q1)
+    sweep(q1, ob, 0, 1, 0, 4, False, True, False, lambda i: None)
+
+    for copy in own2_copies():
+        copy.wait()
+    for copy in north2(NORTH):
+        copy.wait_recv()
 
     @pl.when(low)
     def _():
-        row2_south().start()
-
-    def at_edge_b():
-        edges(1, 1)
-        edges(1, 2)
-
-    def at_rows():
-        row2_north(NORTH).wait_recv()
-
-        @pl.when(low)
-        def _():
-            row2_north(SOUTH).wait_recv()
-
-        halo_q(1, q1)
+        for copy in north2(SOUTH):
+            copy.wait_recv()
+
+    fold(1)
+    row_correction(1)
+    for part in range(3):
+        for copy in col_copies(1, part):
+            copy.wait_recv()
+    for j in range(NJ):
+        edge_correction(1, j)
+
+    OUTS = (2, 4), (10, 4), (6, 4), (14, 2), (0, 2)
 
     def out_copies(part):
-        first, size = ((2, 8), (10, 6), (0, 2))[part]
+        first, size = OUTS[part]
         return [
             pltpu.make_async_copy(
                 ob.at[t, :, pl.ds(first, size), s, :],
@@ -553,33 +662,38 @@
             for s in range(NS)
         ]
 
-    def out_half():
-        for copy in out_copies(0):
-            copy.start()
-
-    edges(1, 0)
-    sweep(q1, ob, 0, 1, at_edge_b, at_rows, out_half)
-    for part in (1, 2):
+    def at_start(i):
+        @pl.when(i == 6)
+        def _():
+            for part in range(2):
+                for copy in out_copies(part):
+                    copy.start()
+
+        restart(q1)(i)
+
+    sweep(q1, ob, 0, 1, 4, 8, False, False, True, at_start)
+    for copy in out_copies(2):
+        copy.start()
+    add_rows(ob, 0)
+    for part in (3, 4):
         for copy in out_copies(part):
             copy.start()
 
-    for copy in north_rows(nslot):
+    for copy in north_rows(nslot) + north2(nslot):
         copy.wait_send()
-    row2_north(nslot).wait_send()
 
     @pl.when(low)
     def _():
-        for copy in south_rows():
+        for copy in south_rows() + south2():
             copy.wait_send()
-        row2_south().wait_send()
 
     for copy in static_col_copies():
         copy.wait_send()
     for step in range(2):
-        for part in range(3):
+        for part in range(len(PARTS[step])):
             for copy in col_copies(step, part):
                 copy.wait_send()
-    for part in range(3):
+    for part in range(len(OUTS)):
         for copy in out_copies(part):
             copy.wait()
 
@@ -587,6 +701,9 @@
 def on_device(t, s, u, v, w, kap, sea, bot):
     def vm(*lead):
         return pltpu.VMEM(lead + (NS, NL), F32)
+
+    def rows(*lead):
+        return pltpu.VMEM(lead + (NK, NL), F32)
 
     def vi(*lead):
         return pltpu.VMEM(lead + (NS, NL), jnp.int32)
@@ -607,10 +724,11 @@
             vm(NK, NJ + 3), vm(NK, NJ + 1), vm(NK, NJ + 1), vm(NK, NJ + 1),
             vm(NK, NJ), vm(NK, NJ), vm(NK, NJ),
             vm(NK, NJ), vm(2, 2, NK), vm(2, 2, NK), vm(2, 2, NK), vm(2, NK), vm(2, NK), vm(2, NK),
-            vm(2, 2, 2, NK, 2), vm(2, NK, 1), vm(2, NK, 1), vi(2, 2), vi(2, 2),
+            rows(2, 2, 4), rows(2, 2, 2, 2), rows(2), rows(2), rows(3), rows(2),
+            pltpu.VMEM((2, 2, NL), jnp.int32), pltpu.VMEM((2, 2, NL), jnp.int32), rows(2, 7), rows(2, 4),
             vm(2, NJ), vm(2, 2, NJ), vm(NJ), vm(2, NJ), vm(), vm(2), vm(NJ),
             vm(2, NJ), vm(2, NJ), vm(2, NJ), vm(2, NJ), vm(2, NJ),
-            dma((8,)), dma((2, NS, 3)), dma((2, 6)), dma((2, 6)), dma((2,)), dma((2,)),
+            dma((8,)), dma((13,)), dma((2, 4)), dma((2, NS, 5)), dma((2, 8)), dma((2, 8)), dma((2, 2, 2)), dma((2, 2, 2)),
             dma((2, 2)), dma((2, 2)), dma((2, 2, 3)), dma((2, 2, 3)),
         ],
         compiler_params=pltpu.CompilerParams(

time: 35.7 us -> 33.7 us (0.944)
  the two profiles are of different devices: /device:TPU:26 before, /device:TPU:2 now
where the time goes in v2:
time: 33.7 us; the launch traced here: 33.6 us
  Pallas kernels  29.6 us (88%)
  local copies, waits for them, and re-layouts  3.36 us (10%)
  between operations  0.65 us (2%)
    pallas_call x1, Pallas kernels, on_device(): pl.pallas_call(kernel, out_shape=(shape, shape), in_specs=[anywhere] * 8,...  29.6 us
    unnamed x4, local copies, waits for them, and re-layouts  3.36 us

profile of v2, /device:TPU:2, one launch (start us, length us, event | category | flops | bytes accessed | tf_op | source)
XLA Modules:
  0.0 33.6 jit_solution(17431095981708900144)
XLA Ops:
  0.6 29.6 %shard_map.95 = (f32[16,128,128]{2,1,0:T(8,128)}, f32[16,128,128]{2,1,0:T(8,128)}) custom-call(f32[16,128,128]{2,1,0:T(8,128)} %t_hbm.1, f32[16,128,128]{2,1,0:T(8,128)} %s_hbm.1, f32[16,128,128]{2,1,0:T(8,128)} %u_hbm.1, f32[16,128,128]{2,1,0:T(8,128)} %v_hbm.1, f32[16,128,128]{2,1,0:T(8,128)} %w_hbm.1, f32[16,128,128]{2,1,0:T(8,128)} %k_hbm.1, ...), custom_call_target="tpu_custom_call" | custom-call | flops 120000000 | bytes 9000000 | tf_op jit(solution)/shard_map/pallas_call | solution.py:714
  30.2 0.0 copy-start
  30.2 2.4 %copy.12 = f32[16,128,128]{2,1,0:T(8,128)} copy(f32[16,128,128]{2,1,0:T(8,128)} %get-tuple-element.4) | data formatting | bytes 2097152
  32.6 0.0 copy-done
  32.6 1.0 %copy.13 = f32[16,128,128]{2,1,0:T(8,128)} copy(f32[16,128,128]{2,1,0:T(8,128)S(1)} %copy-done) | data formatting | bytes 2097152
Async XLA Ops:
  30.2 2.4 %copy-start = (f32[16,128,128]{2,1,0:T(8,128)S(1)}, f32[16,128,128]{2,1,0:T(8,128)}, u32[]{:S(2)}) copy-start(f32[16,128,128]{2,1,0:T(8,128)} %get-tuple-element.5) | copy-start | bytes 3145732

commit v3 on v2

--- a/solution.py
+++ b/solution.py
@@ -32,7 +32,7 @@
     ox, sx, bx, ex, oy, sy, by, ey, oz, sz, ez,
     oxw, dx, hx, fx, dy, hy, fy,
     rown, rhal, rk, rkh, rv, rvh, hs, hb, rcoef, rc,
-    pq, pr, uko, ukr, flo, flr, cc,
+    pq, pr, sent, uko, sent_uk, got_uk, sent_k, got_k, flo, flr, cc,
     eo, es, eb, ec, ed,
     in_sem, own_sem, own2_sem, out_sem, row_send, row_recv, row2_send, row2_recv,
     col_send, col_recv, col2_send, col2_recv,
@@ -64,22 +64,22 @@
     def _():
         pl.semaphore_signal(barrier, inc=1, device_id=south, device_id_type=mesh_ids)
 
-    def load(index, src, dst3, lead):
-        for s in range(NS):
-            rows = pl.ds(NJ * s, NJ)
-            if lead:
-                pltpu.make_async_copy(src.at[:, rows, :], dst3(s), in_sem.at[index]).start()
-            else:
-                pltpu.make_async_copy(src.at[rows, :], dst3(s), in_sem.at[index]).start()
-
-    load(0, t_hbm, lambda s: q0.at[0, :, pl.ds(2, NJ), s, :], True)
-    load(1, s_hbm, lambda s: q0.at[1, :, pl.ds(2, NJ), s, :], True)
-    load(2, sea_hbm, lambda s: seab.at[pl.ds(2, NJ), s, :], False)
-    load(3, bot_hbm, lambda s: botb.at[pl.ds(2, NJ), s, :], False)
-    load(4, u_hbm, lambda s: ub.at[:, :, s, :], True)
-    load(5, k_hbm, lambda s: kb.at[:, pl.ds(1, NJ), s, :], True)
-    load(6, v_hbm, lambda s: vb.at[:, pl.ds(1, NJ), s, :], True)
-    load(7, w_hbm, lambda s: wb.at[:, :, s, :], True)
+    @pl.loop(0, NS)
+    def _(s):
+        rows = pl.ds(pl.multiple_of(NJ * s, NJ), NJ)
+        inner = pl.ds(2, NJ)
+        inner1 = pl.ds(1, NJ)
+        for index, (src, dst) in enumerate((
+            (t_hbm.at[:, rows, :], q0.at[0, :, inner, s, :]),
+            (s_hbm.at[:, rows, :], q0.at[1, :, inner, s, :]),
+            (sea_hbm.at[rows, :], seab.at[inner, s, :]),
+            (bot_hbm.at[rows, :], botb.at[inner, s, :]),
+            (u_hbm.at[:, rows, :], ub.at[:, :, s, :]),
+            (k_hbm.at[:, rows, :], kb.at[:, inner1, s, :]),
+            (v_hbm.at[:, rows, :], vb.at[:, inner1, s, :]),
+            (w_hbm.at[:, rows, :], wb.at[:, :, s, :]),
+        )):
+            pltpu.make_async_copy(src, dst, in_sem.at[index]).start()
 
     def loaded(index, whole):
         pltpu.make_async_copy(whole, whole, in_sem.at[index]).wait()
@@ -136,20 +136,48 @@
             acc = jnp.where(group == n, moved, acc)
         return acc
 
-    PARTS = ((0, NJ),), ((2, NJ - 4), (NJ - 2, 2), (0, 2))
+    PARTS = ((0, NJ // 2),), ((2, NJ // 2 - 4), (NJ // 2 - 2, 2), (0, 2))
+
+    def squeeze(step, rows):
+        pair = lane & 63
+        index = 4 * (pair >> 1) + (pair & 1)
+        first = lane < NL // 2
+        for a in rows:
+            for side in (EAST, WEST):
+                at = index + (2 if side == WEST else 0)
+                sent[step, side, a] = jnp.where(
+                    first,
+                    jnp.take_along_axis(pq[step, a], at, axis=1),
+                    jnp.take_along_axis(pq[step, a + NJ // 2], at, axis=1),
+                )
 
     def col_copies(step, part):
         first, size = PARTS[step][part]
         sl = pl.ds(first, size)
         return [
-            remote(pq.at[step, sl], pr.at[step, EAST, sl], col2_send.at[step, 0, part], col2_recv.at[step, EAST, part], west),
-            remote(pq.at[step, sl], pr.at[step, WEST, sl], col2_send.at[step, 1, part], col2_recv.at[step, WEST, part], east),
+            remote(sent.at[step, WEST, sl], pr.at[step, EAST, sl], col2_send.at[step, 0, part], col2_recv.at[step, EAST, part], west),
+            remote(sent.at[step, EAST, sl], pr.at[step, WEST, sl], col2_send.at[step, 1, part], col2_recv.at[step, WEST, part], east),
         ]
+
+    def squeeze_static():
+        quarter = lane & 31
+        to_east = 4 * quarter + 1
+        to_west = NL // 2 + 4 * (lane & 15) + 2
+        for m in range(4):
+            acc = jnp.take_along_axis(uko[m], to_east, axis=1)
+            for n in range(1, 4):
+                acc = jnp.where((lane >> 5) == n, jnp.take_along_axis(uko[m + 4 * n], to_east, axis=1), acc)
+            sent_uk[m] = acc
+        for m in range(2):
+            acc = jnp.take_along_axis(uko[m], to_west, axis=1)
+            for n in range(1, 8):
+                acc = jnp.where((lane >> 4) == n, jnp.take_along_axis(uko[m + 2 * n], to_west, axis=1), acc)
+            sent_k[m] = acc
 
     def static_col_copies():
         return [
-            remote(uko, ukr.at[EAST], col_send.at[0, 0], col_recv.at[EAST, 0], west),
-            remote(uko, ukr.at[WEST], col_send.at[1, 0], col_recv.at[WEST, 0], east),
+            remote(sent_k, got_k, col_send.at[0, 0], col_recv.at[EAST, 0], west),
+            remote(sent_uk, got_uk, col_send.at[1, 0], col_recv.at[WEST, 0], east),
             remote(flo, flr.at[EAST], col_send.at[0, 1], col_recv.at[EAST, 1], west),
             remote(flo, flr.at[WEST], col_send.at[1, 1], col_recv.at[WEST, 1], east),
         ]
@@ -157,10 +185,10 @@
     loaded(0, q0.at[0, :, pl.ds(2, NJ)])
     loaded(1, q0.at[1, :, pl.ds(2, NJ)])
 
-    @pl.loop(0, NJ // 4)
-    def _(quarter):
-        for h in range(4):
-            j = 4 * quarter + h
+    @pl.loop(0, NJ // 2)
+    def _(half):
+        for h in range(2):
+            j = 2 * half + h
             pq[0, j] = pack(lambda n: q0[n // NK, n % NK, j + 2], 2 * NK)
 
     loaded(2, seab.at[pl.ds(2, NJ)])
@@ -171,12 +199,6 @@
     loaded(4, ub)
     loaded(5, kb.at[:, pl.ds(1, NJ)])
 
-    @pl.loop(0, NJ // 4)
-    def _(quarter):
-        for h in range(4):
-            j = 4 * quarter + h
-            uko[j] = pack(lambda n: ub[n, j] if n < NK else kb[n - NK, j + 1], 2 * NK)
-
     def first_sends():
         pl.semaphore_wait(barrier, jnp.where(low, 4, 3))
         for copy in col_copies(0, 0):
@@ -212,6 +234,7 @@
     def _(j):
         fl = flb[j + 2]
         face = jnp.where(lane == NL - 1, 0.0, jnp.minimum(fl, pltpu.roll(fl, NL - 1, 1)))
+        uko[j] = pack(lambda n: ub[n, j] if n < NK else kb[n - NK, j + 1], 2 * NK)
         face_w = jnp.where(lane == 0, 0.0, jnp.minimum(fl, pltpu.roll(fl, 1, 1)))
         for k in range(NK):
             is_open = face > k
@@ -229,11 +252,6 @@
                 sz[k, j] = jnp.where(below, w, 0.0)
                 ez[k, j] = quarter_edge(w)
 
-    @pl.loop(0, NJ - 1)
-    def _(j):
-        open_y(j)
-        coef_y(j)
-
     for r in range(2):
         flb[r] = jnp.where(sub == 0, 0.0, pltpu.roll(flb[NJ + r], 1, 0))
         flb[NJ + 2 + r] = jnp.where(sub == NS - 1, 0.0, pltpu.roll(flb[2 + r], NS - 1, 0))
@@ -241,20 +259,30 @@
         kb[k, 0] = pltpu.roll(kb[k, NJ], 1, 0)
         kb[k, NJ + 1] = pltpu.roll(kb[k, 1], NS - 1, 0)
         vb[k, 0] = pltpu.roll(vb[k, NJ], 1, 0)
-    for j in (-2, -1, NJ - 1, NJ):
-        open_y(j)
-    for j in (-1, NJ - 1):
-        coef_y(j)
+
+    @pl.loop(0, NJ + 1)
+    def _(j):
+        open_y(j - 1)
+        coef_y(j - 1)
+
+    @pl.loop(0, 2)
+    def _(r):
+        open_y((NJ + 2) * r - 2)
 
     def wrap_rows(q):
-        for t in range(2):
-            for k in range(NK):
-                for r in range(2):
-                    q[t, k, r] = pltpu.roll(q[t, k, NJ + r], 1, 0)
-                    q[t, k, NJ + 2 + r] = pltpu.roll(q[t, k, 2 + r], NS - 1, 0)
-
+        @pl.loop(0, NK // 4)
+        def _(kk):
+            for k4 in range(4):
+                k = 4 * kk + k4
+                for t in range(2):
+                    for r in range(2):
+                        q[t, k, r] = pltpu.roll(q[t, k, NJ + r], 1, 0)
+                        q[t, k, NJ + 2 + r] = pltpu.roll(q[t, k, 2 + r], NS - 1, 0)
+
+    squeeze(0, range(NJ // 2))
+    squeeze_static()
+    first_sends()
     wrap_rows(q0)
-    first_sends()
 
     def mirror(x):
         return jnp.take_along_axis(x, NL - 1 - lane, axis=1)
@@ -349,10 +377,15 @@
                         rc[t, 3, lv, :] = g - f
 
     def add_rows(out, off):
-        for a, (j, s) in enumerate(((0, 0), (1, 0), (NJ - 2, NS - 1), (NJ - 1, NS - 1))):
-            for t in range(2):
-                for k in range(NK):
-                    out[t, k, j + off, s : s + 1, :] = out[t, k, j + off, s : s + 1, :] + rc[t, a, k : k + 1, :]
+        @pl.loop(0, NK // 4)
+        def _(kk):
+            for k4 in range(4):
+                k = 4 * kk + k4
+                for a, (j, s) in enumerate(((0, 0), (1, 0), (NJ - 2, NS - 1), (NJ - 1, NS - 1))):
+                    for t in range(2):
+                        out[t, k, j + off, s : s + 1, :] = (
+                            out[t, k, j + off, s : s + 1, :] + rc[t, a, pl.ds(k, 1), :]
+                        )
 
     def wait_rows(slot):
         for copy in row_copies(0, 0, slot, 0, north):
@@ -361,21 +394,29 @@
     level4 = (group & (NK - 1)).astype(F32)
 
     def edge_static():
-        for j in range(NJ):
+        @pl.loop(0, NJ // 4)
+        def _(quarter):
+          for h in range(4):
+            j = 4 * quarter + h
             index = 4 * j + l4
 
             def spread(x):
                 return jnp.take_along_axis(x, index, axis=1)
 
             own_f, east_f, west_f = spread(flo[...]), spread(flr[EAST]), spread(flr[WEST])
+
+            level = group & (NK - 1)
+            west_uk = got_uk[j & 3]
+            west_at = 32 * (j >> 2) + level
+            west_u = jnp.take_along_axis(west_uk, west_at, axis=1)
+            west_k = jnp.take_along_axis(west_uk, west_at + NK, axis=1)
+            east_k = jnp.take_along_axis(got_k[j & 1], NK * (j >> 1) + level, axis=1)
 
             def halves(x):
                 other = pltpu.roll(x, NL // 2, 1)
                 return jnp.where(lane < NL // 2, x, other), jnp.where(lane < NL // 2, other, x)
 
             own_u, own_k = halves(uko[j])
-            _, east_k = halves(ukr[EAST, j])
-            west_u, west_k = halves(ukr[WEST, j])
             first = l4 < 2
             for side in (EAST, WEST):
                 if side == EAST:
@@ -405,17 +446,23 @@
         own = pq[step, j]
         first = l4 < 2
         sums = []
+        at = 2 * group + (lane & 1) + (NL // 2 if j >= NJ // 2 else 0)
+        a = j % (NJ // 2)
         for side in (EAST, WEST):
             if side == EAST:
-                win = jnp.where(first, own, pr[step, EAST, j])
+                win = jnp.where(first, own, jnp.take_along_axis(pr[step, EAST, a], at, axis=1))
             else:
-                win = jnp.where(first, pr[step, WEST, j], own)
+                win = jnp.where(first, jnp.take_along_axis(pr[step, WEST, a], at, axis=1), own)
             d = (pltpu.roll(win, NL - 1, 1) - win) * eo[side, j]
             before = pltpu.roll(d, 1, 1)
             h = limiter(0.25 * (d + before), before, d)
             g = es[side, j] * win + eb[side, j] * d + ec[side, j] * h + ed[side, j] * pltpu.roll(h, NL - 1, 1)
             sums.append(pltpu.roll(g, 1, 1) - g)
         cc[j] = jnp.where(first, sums[EAST], sums[WEST])
+
+    def edge_corrections(step):
+        for j in range(NJ):
+            edge_correction(step, j)
 
     def unpacked(j, n):
         return jnp.where(edge_lanes, pltpu.roll(cc[j], (NL - 2 - 4 * n) % NL, 1), 0.0)
@@ -555,7 +602,6 @@
 
         return at
 
-    outer = (NJ - 2, NJ - 1, 0, 1)
     start_sweep(q0)
     sweep(q0, q1, 2, 0, 0, 8, True, False, False, restart(q0))
 
@@ -575,15 +621,19 @@
     for copy in col_copies(0, 0):
         copy.wait_recv()
     edge_static()
-    for j in range(NJ):
-        edge_correction(0, j)
+    edge_corrections(0)
     for j in range(2, NJ - 2):
         pq[1, j] = pq[1, j] + cc[j]
+    squeeze(1, range(2, NJ // 2 - 2))
     for copy in col_copies(1, 0):
         copy.start()
     add_rows(q1, 2)
-    for j in outer:
-        add_columns(q1, 2, j)
+
+    @pl.loop(0, 2)
+    def _(half):
+        for h in range(2):
+            add_columns(q1, 2, (2 * half + h + NJ - 2) & (NJ - 1))
+
 
     def row2_copies(j, s, slot, direction, device):
         return [
@@ -618,14 +668,22 @@
 
     for copy in own2_copies():
         copy.start()
-    for j in outer:
-        repack(q1, 2, j)
+
+    @pl.loop(0, 2)
+    def _(half):
+        for h in range(2):
+            repack(q1, 2, (2 * half + h + NJ - 2) & (NJ - 1))
+
+    squeeze(1, (0, 1, NJ // 2 - 2, NJ // 2 - 1))
     for part in (1, 2):
         for copy in col_copies(1, part):
             copy.start()
 
-    for j in (2, 3, 4, NJ - 3):
-        add_columns(q1, 2, j)
+    @pl.loop(0, 2)
+    def _(half):
+        for h in range(2):
+            add_columns(q1, 2, 2 + h + half * (2 + 8 * h))
+
     wrap_rows(q1)
     start_sweep(q1)
     sweep(q1, ob, 0, 1, 0, 4, False, True, False, lambda i: None)
@@ -645,39 +703,41 @@
     for part in range(3):
         for copy in col_copies(1, part):
             copy.wait_recv()
-    for j in range(NJ):
-        edge_correction(1, j)
+    edge_corrections(1)
 
     OUTS = (2, 4), (10, 4), (6, 4), (14, 2), (0, 2)
 
-    def out_copies(part):
+    def out_start(part):
         first, size = OUTS[part]
-        return [
-            pltpu.make_async_copy(
-                ob.at[t, :, pl.ds(first, size), s, :],
-                dst.at[:, pl.ds(NJ * s + first, size), :],
-                out_sem.at[t, s, part],
-            )
-            for t, dst in enumerate((tout_hbm, sout_hbm))
-            for s in range(NS)
-        ]
+
+        @pl.loop(0, NS)
+        def _(s):
+            for t, dst in enumerate((tout_hbm, sout_hbm)):
+                pltpu.make_async_copy(
+                    ob.at[t, :, pl.ds(first, size), s, :],
+                    dst.at[:, pl.ds(NJ * s + first, size), :],
+                    out_sem.at[t, part],
+                ).start()
+
+    def out_wait(part):
+        first, size = OUTS[part]
+        for t in range(2):
+            whole = ob.at[t, :, pl.ds(first, size)]
+            pltpu.make_async_copy(whole, whole, out_sem.at[t, part]).wait()
 
     def at_start(i):
         @pl.when(i == 6)
         def _():
             for part in range(2):
-                for copy in out_copies(part):
-                    copy.start()
+                out_start(part)
 
         restart(q1)(i)
 
     sweep(q1, ob, 0, 1, 4, 8, False, False, True, at_start)
-    for copy in out_copies(2):
-        copy.start()
+    out_start(2)
     add_rows(ob, 0)
     for part in (3, 4):
-        for copy in out_copies(part):
-            copy.start()
+        out_start(part)
 
     for copy in north_rows(nslot) + north2(nslot):
         copy.wait_send()
@@ -694,8 +754,24 @@
             for copy in col_copies(step, part):
                 copy.wait_send()
     for part in range(len(OUTS)):
-        for copy in out_copies(part):
-            copy.wait()
+        out_wait(part)
+
+
+def hand_over(t_in, s_in, t_out, s_out, held, in_sem, out_sem):
+    pieces = [
+        (src.at[pl.ds(4 * n, 4)], held.at[a, pl.ds(4 * n, 4)], dst.at[pl.ds(4 * n, 4)], a, n)
+        for n in range(4)
+        for a, (src, dst) in enumerate(((t_in, t_out), (s_in, s_out)))
+    ]
+    reads = [pltpu.make_async_copy(src, mid, in_sem.at[a, n]) for src, mid, dst, a, n in pieces]
+    writes = [pltpu.make_async_copy(mid, dst, out_sem.at[a, n]) for src, mid, dst, a, n in pieces]
+    for copy in reads:
+        copy.start()
+    for read, write in zip(reads, writes):
+        read.wait()
+        write.start()
+    for copy in writes:
+        copy.wait()
 
 
 def on_device(t, s, u, v, w, kap, sea, bot):
@@ -711,7 +787,7 @@
     dma = pltpu.SemaphoreType.DMA
     anywhere = pl.BlockSpec(memory_space=pl.ANY)
     shape = jax.ShapeDtypeStruct(t.shape, F32)
-    return pl.pallas_call(
+    held = pl.pallas_call(
         kernel,
         out_shape=(shape, shape),
         in_specs=[anywhere] * 8,
@@ -726,9 +802,9 @@
             vm(NK, NJ), vm(2, 2, NK), vm(2, 2, NK), vm(2, 2, NK), vm(2, NK), vm(2, NK), vm(2, NK),
             rows(2, 2, 4), rows(2, 2, 2, 2), rows(2), rows(2), rows(3), rows(2),
             pltpu.VMEM((2, 2, NL), jnp.int32), pltpu.VMEM((2, 2, NL), jnp.int32), rows(2, 7), rows(2, 4),
-            vm(2, NJ), vm(2, 2, NJ), vm(NJ), vm(2, NJ), vm(), vm(2), vm(NJ),
+            vm(2, NJ), vm(2, 2, NJ // 2), vm(2, 2, NJ // 2), vm(NJ), vm(4), vm(4), vm(2), vm(2), vm(), vm(2), vm(NJ),
             vm(2, NJ), vm(2, NJ), vm(2, NJ), vm(2, NJ), vm(2, NJ),
-            dma((8,)), dma((13,)), dma((2, 4)), dma((2, NS, 5)), dma((2, 8)), dma((2, 8)), dma((2, 2, 2)), dma((2, 2, 2)),
+            dma((8,)), dma((13,)), dma((2, 4)), dma((2, 5)), dma((2, 8)), dma((2, 8)), dma((2, 2, 2)), dma((2, 2, 2)),
             dma((2, 2)), dma((2, 2)), dma((2, 2, 3)), dma((2, 2, 3)),
         ],
         compiler_params=pltpu.CompilerParams(
@@ -736,6 +812,14 @@
         ),
         cost_estimate=pl.CostEstimate(flops=120_000_000, bytes_accessed=9_000_000, transcendentals=0),
     )(t, s, u, v, w, kap, sea, bot)
+    return pl.pallas_call(
+        hand_over,
+        out_shape=(shape, shape),
+        in_specs=[anywhere] * 2,
+        out_specs=(anywhere, anywhere),
+        scratch_shapes=[pltpu.VMEM((2,) + t.shape, F32), dma((2, 4)), dma((2, 4))],
+        compiler_params=pltpu.CompilerParams(vmem_limit_bytes=60 * 1024 * 1024),
+    )(*held)
 
 
 def solution(mesh):

time: 33.7 us -> 31.4 us (0.932)
  the two profiles are of different devices: /device:TPU:2 before, /device:TPU:16 now
where the time goes in v3:
time: 31.4 us; the launch traced here: 31.2 us
  Pallas kernels  30.6 us (97%)
  between operations  0.64 us (2%)
    pallas_call x1, Pallas kernels, on_device(): pl.pallas_call(kernel, out_shape=(shape, shape), in_specs=[anywhere] * 8,...  28.2 us
    pallas_call x1, Pallas kernels, on_device(): pl.pallas_call(hand_over, out_shape=(shape, shape), in_specs=[anywhere] *...  2.39 us

profile of v3, /device:TPU:16, one launch (start us, length us, event | category | flops | bytes accessed | tf_op | source)
XLA Modules:
  0.0 31.2 jit_solution(18103621382044887972)
XLA Ops:
  0.6 28.2 %shard_map.95 = (f32[16,128,128]{2,1,0:T(8,128)}, f32[16,128,128]{2,1,0:T(8,128)}) custom-call(f32[16,128,128]{2,1,0:T(8,128)} %t_hbm.1, f32[16,128,128]{2,1,0:T(8,128)} %s_hbm.1, f32[16,128,128]{2,1,0:T(8,128)} %u_hbm.1, f32[16,128,128]{2,1,0:T(8,128)} %v_hbm.1, f32[16,128,128]{2,1,0:T(8,128)} %w_hbm.1, f32[16,128,128]{2,1,0:T(8,128)} %k_hbm.1, ...), custom_call_target="tpu_custom_call" | custom-call | flops 120000000 | bytes 9000000 | tf_op jit(solution)/shard_map/pallas_call | solution.py:790
  28.9 2.4 %shard_map.96 = (f32[16,128,128]{2,1,0:T(8,128)}, f32[16,128,128]{2,1,0:T(8,128)}) custom-call(f32[16,128,128]{2,1,0:T(8,128)} %get-tuple-element.4.t_in, f32[16,128,128]{2,1,0:T(8,128)} %get-tuple-element.5.s_in), custom_call_target="tpu_custom_call" | custom-call | tf_op jit(solution)/shard_map/pallas_call | solution.py:815

commit v4 on v3

--- a/solution.py
+++ b/solution.py
@@ -211,8 +211,7 @@
             for copy in south_rows():
                 copy.start()
 
-        for copy in static_col_copies():
-            copy.start()
+    squeeze(0, range(NJ // 2))
 
     loaded(6, vb.at[:, pl.ds(1, NJ)])
     loaded(7, wb)
@@ -232,6 +231,10 @@
 
     @pl.loop(0, NJ)
     def _(j):
+        @pl.when(j == NJ // 2)
+        def _():
+            first_sends()
+
         fl = flb[j + 2]
         face = jnp.where(lane == NL - 1, 0.0, jnp.minimum(fl, pltpu.roll(fl, NL - 1, 1)))
         uko[j] = pack(lambda n: ub[n, j] if n < NK else kb[n - NK, j + 1], 2 * NK)
@@ -252,6 +255,10 @@
                 sz[k, j] = jnp.where(below, w, 0.0)
                 ez[k, j] = quarter_edge(w)
 
+    squeeze_static()
+    for copy in static_col_copies():
+        copy.start()
+
     for r in range(2):
         flb[r] = jnp.where(sub == 0, 0.0, pltpu.roll(flb[NJ + r], 1, 0))
         flb[NJ + 2 + r] = jnp.where(sub == NS - 1, 0.0, pltpu.roll(flb[2 + r], NS - 1, 0))
@@ -279,9 +286,6 @@
                         q[t, k, r] = pltpu.roll(q[t, k, NJ + r], 1, 0)
                         q[t, k, NJ + 2 + r] = pltpu.roll(q[t, k, 2 + r], NS - 1, 0)
 
-    squeeze(0, range(NJ // 2))
-    squeeze_static()
-    first_sends()
     wrap_rows(q0)
 
     def mirror(x):
@@ -394,10 +398,10 @@
     level4 = (group & (NK - 1)).astype(F32)
 
     def edge_static():
-        @pl.loop(0, NJ // 4)
-        def _(quarter):
-          for h in range(4):
-            j = 4 * quarter + h
+        @pl.loop(0, NJ // 8)
+        def _(half):
+          for h in range(8):
+            j = 8 * half + h
             index = 4 * j + l4
 
             def spread(x):
@@ -504,10 +508,10 @@
         pq[1, j] = (sums[0] + sums[1]) + (sums[2] + sums[3])
 
     def meridional_start(q, j):
-        @pl.loop(0, NK // 4)
+        @pl.loop(0, NK // 8)
         def _(kk):
-            for k4 in range(4):
-                k = 4 * kk + k4
+            for k4 in range(8):
+                k = 8 * kk + k4
                 s, b, e = sy[k, j], by[k, j], ey[k, j]
                 for t in range(2):
                     a2, a1, c0, c1 = (q[t, k, j + n] for n in range(4))
@@ -586,7 +590,8 @@
                 if fixing_in:
                     add_columns(q, 2, j + 3)
                 if fixing_out:
-                    add_columns(out, off, (j - NJ // 2) & (NJ - 1))
+                    for n in range(3):
+                        add_columns(out, off, 2 + 3 * ((j + 2) & (NJ - 1)) + n)
 
     def start_sweep(q):
         zonal_slopes(q, 2, 0)
@@ -679,17 +684,23 @@
         for copy in col_copies(1, part):
             copy.start()
 
-    @pl.loop(0, 2)
-    def _(half):
-        for h in range(2):
-            add_columns(q1, 2, 2 + h + half * (2 + 8 * h))
+    for j in (NJ - 2, NJ - 1, NJ):
+        cc[j] = jnp.zeros((NS, NL), F32)
+    for j in (2, 3, 4):
+        add_columns(q1, 2, j)
 
     wrap_rows(q1)
     start_sweep(q1)
-    sweep(q1, ob, 0, 1, 0, 4, False, True, False, lambda i: None)
-
-    for copy in own2_copies():
-        copy.wait()
+
+    def rows_left(i):
+        @pl.when(i == 4)
+        def _():
+            for copy in own2_copies():
+                copy.wait()
+            for copy in north2(nslot):
+                copy.wait_send()
+
+    sweep(q1, ob, 0, 1, 0, 6, False, True, False, rows_left)
     for copy in north2(NORTH):
         copy.wait_recv()
 
@@ -705,7 +716,7 @@
             copy.wait_recv()
     edge_corrections(1)
 
-    OUTS = (2, 4), (10, 4), (6, 4), (14, 2), (0, 2)
+    OUTS = (2, 6), (8, 6), (14, 2), (0, 2)
 
     def out_start(part):
         first, size = OUTS[part]
@@ -726,20 +737,19 @@
             pltpu.make_async_copy(whole, whole, out_sem.at[t, part]).wait()
 
     def at_start(i):
-        @pl.when(i == 6)
+        @pl.when(i == 7)
         def _():
-            for part in range(2):
-                out_start(part)
+            out_start(0)
 
         restart(q1)(i)
 
-    sweep(q1, ob, 0, 1, 4, 8, False, False, True, at_start)
-    out_start(2)
+    sweep(q1, ob, 0, 1, 6, 8, False, False, True, at_start)
+    out_start(1)
     add_rows(ob, 0)
-    for part in (3, 4):
+    for part in (2, 3):
         out_start(part)
 
-    for copy in north_rows(nslot) + north2(nslot):
+    for copy in north_rows(nslot):
         copy.wait_send()
 
     @pl.when(low)
@@ -802,7 +812,7 @@
             vm(NK, NJ), vm(2, 2, NK), vm(2, 2, NK), vm(2, 2, NK), vm(2, NK), vm(2, NK), vm(2, NK),
             rows(2, 2, 4), rows(2, 2, 2, 2), rows(2), rows(2), rows(3), rows(2),
             pltpu.VMEM((2, 2, NL), jnp.int32), pltpu.VMEM((2, 2, NL), jnp.int32), rows(2, 7), rows(2, 4),
-            vm(2, NJ), vm(2, 2, NJ // 2), vm(2, 2, NJ // 2), vm(NJ), vm(4), vm(4), vm(2), vm(2), vm(), vm(2), vm(NJ),
+            vm(2, NJ), vm(2, 2, NJ // 2), vm(2, 2, NJ // 2), vm(NJ), vm(4), vm(4), vm(2), vm(2), vm(), vm(2), vm(NJ + 1),
             vm(2, NJ), vm(2, NJ), vm(2, NJ), vm(2, NJ), vm(2, NJ),
             dma((8,)), dma((13,)), dma((2, 4)), dma((2, 5)), dma((2, 8)), dma((2, 8)), dma((2, 2, 2)), dma((2, 2, 2)),
             dma((2, 2)), dma((2, 2)), dma((2, 2, 3)), dma((2, 2, 3)),

time: 31.4 us -> 30.2 us (0.962)
  Pallas kernels: 30.6 us -> 29.4 us
    pallas_call x1, Pallas kernels: 28.2 us -> 27 us  [on_device(): pl.pallas_call(kernel, out_shape=(shape, shape), in_specs=[anywhere] * 8,...]
where the time goes in v4:
time: 30.2 us; the launch traced here: 30 us
  Pallas kernels  29.4 us (97%)
  between operations  0.64 us (2%)
    pallas_call x1, Pallas kernels, on_device(): pl.pallas_call(kernel, out_shape=(shape, shape), in_specs=[anywhere] * 8,...  27 us
    pallas_call x1, Pallas kernels, on_device(): pl.pallas_call(hand_over, out_shape=(shape, shape), in_specs=[anywhere] *...  2.39 us

profile of v4, /device:TPU:16, one launch (start us, length us, event | category | flops | bytes accessed | tf_op | source)
XLA Modules:
  0.0 30.0 jit_solution(17835374735334477261)
XLA Ops:
  0.6 27.0 %shard_map.95 = (f32[16,128,128]{2,1,0:T(8,128)}, f32[16,128,128]{2,1,0:T(8,128)}) custom-call(f32[16,128,128]{2,1,0:T(8,128)} %t_hbm.1, f32[16,128,128]{2,1,0:T(8,128)} %s_hbm.1, f32[16,128,128]{2,1,0:T(8,128)} %u_hbm.1, f32[16,128,128]{2,1,0:T(8,128)} %v_hbm.1, f32[16,128,128]{2,1,0:T(8,128)} %w_hbm.1, f32[16,128,128]{2,1,0:T(8,128)} %k_hbm.1, ...), custom_call_target="tpu_custom_call" | custom-call | flops 120000000 | bytes 9000000 | tf_op jit(solution)/shard_map/pallas_call | solution.py:800
  27.6 2.4 %shard_map.96 = (f32[16,128,128]{2,1,0:T(8,128)}, f32[16,128,128]{2,1,0:T(8,128)}) custom-call(f32[16,128,128]{2,1,0:T(8,128)} %get-tuple-element.4.t_in, f32[16,128,128]{2,1,0:T(8,128)} %get-tuple-element.5.s_in), custom_call_target="tpu_custom_call" | custom-call | tf_op jit(solution)/shard_map/pallas_call | solution.py:825

commit v5 on v4

--- a/solution.py
+++ b/solution.py
@@ -231,7 +231,7 @@
 
     @pl.loop(0, NJ)
     def _(j):
-        @pl.when(j == NJ // 2)
+        @pl.when(j == NJ // 4)
         def _():
             first_sends()
 
@@ -769,8 +769,8 @@
 
 def hand_over(t_in, s_in, t_out, s_out, held, in_sem, out_sem):
     pieces = [
-        (src.at[pl.ds(4 * n, 4)], held.at[a, pl.ds(4 * n, 4)], dst.at[pl.ds(4 * n, 4)], a, n)
-        for n in range(4)
+        (src.at[pl.ds(8 * n, 8)], held.at[a, pl.ds(8 * n, 8)], dst.at[pl.ds(8 * n, 8)], a, n)
+        for n in range(2)
         for a, (src, dst) in enumerate(((t_in, t_out), (s_in, s_out)))
     ]
     reads = [pltpu.make_async_copy(src, mid, in_sem.at[a, n]) for src, mid, dst, a, n in pieces]

time: 30.2 us -> 30.3 us (level)
  no operation moved by 1% of the time
where the time goes in v5:
time: 30.3 us; the launch traced here: 30.1 us
  Pallas kernels  29.5 us (97%)
  between operations  0.64 us (2%)
    pallas_call x1, Pallas kernels, on_device(): pl.pallas_call(kernel, out_shape=(shape, shape), in_specs=[anywhere] * 8,...  27 us
    pallas_call x1, Pallas kernels, on_device(): pl.pallas_call(hand_over, out_shape=(shape, shape), in_specs=[anywhere] *...  2.49 us

profile of v5, /device:TPU:16, one launch (start us, length us, event | category | flops | bytes accessed | tf_op | source)
XLA Modules:
  0.0 30.1 jit_solution(11840191528815036380)
XLA Ops:
  0.6 27.0 %shard_map.95 = (f32[16,128,128]{2,1,0:T(8,128)}, f32[16,128,128]{2,1,0:T(8,128)}) custom-call(f32[16,128,128]{2,1,0:T(8,128)} %t_hbm.1, f32[16,128,128]{2,1,0:T(8,128)} %s_hbm.1, f32[16,128,128]{2,1,0:T(8,128)} %u_hbm.1, f32[16,128,128]{2,1,0:T(8,128)} %v_hbm.1, f32[16,128,128]{2,1,0:T(8,128)} %w_hbm.1, f32[16,128,128]{2,1,0:T(8,128)} %k_hbm.1, ...), custom_call_target="tpu_custom_call" | custom-call | flops 120000000 | bytes 9000000 | tf_op jit(solution)/shard_map/pallas_call | solution.py:800
  27.6 2.5 %shard_map.96 = (f32[16,128,128]{2,1,0:T(8,128)}, f32[16,128,128]{2,1,0:T(8,128)}) custom-call(f32[16,128,128]{2,1,0:T(8,128)} %get-tuple-element.4.t_in, f32[16,128,128]{2,1,0:T(8,128)} %get-tuple-element.5.s_in), custom_call_target="tpu_custom_call" | custom-call | tf_op jit(solution)/shard_map/pallas_call | solution.py:825
